TPU v7x, 32 devices: a whole 2x2x4 slice. The times are simulated.
32 devices in a mesh: group: 2 (over y), cuts: 4 (over z), probe: 4 (over x, core).
Axes of the slice: x: 2, y: 2, z: 4, core: 2. Of those that a mesh axis runs over, the one named last changes fastest.
Arguments:
- object_slices: float32 [2, 8, 384, 384], P(None, ('group', 'cuts')), parts along dimension 1, may hold values from -1 to 1, as said below
- probe: bfloat16 [4, 128, 128], P('group'), parts along dimension 0, may hold values from -4 to 4
- intensities: float32 [64, 128, 128], P(('group', 'probe')), parts along dimension 0, may hold values from 0.05 to 2
- offsets: int32 [64, 2], P(('group', 'probe')), parts along dimension 0, may hold values from 0 to 256
Outputs:
- object_new: float32 [2, 8, 384, 384], P(None, ('group', 'cuts')), parts along dimension 1
There are 2 independent parts, one for each index of `group`. A program takes and returns all parts, laid end to end along the dimension named above; each array names one. Nothing has to cross between parts.
Inputs may be any that keep to these rules, and one draw needn't show every extreme that they name: `object_slices`: each cell's two components form a complex number of magnitude between exp(-0.8 / 4) and 1.
All inputs are finite; a program needn't handle non-finite values.
Results may differ from a plain program's by a relative error of at most 0.0028.
Values may be sent and summed in bfloat16 or wider, within the bound.
No kernel may reach another device: no remote copies, remote signals or barrier semaphores. Data moves between devices by JAX's collectives and lax.ppermute only.
A program may use at most 64 MiB of HBM per device.

v0:
```python
import math

import jax
import jax.numpy as jnp
from jax import lax
from jax.sharding import PartitionSpec as P

fresnel_phase = 12.0
step_size = 0.5
regular = 1.0
highest = lax.Precision.HIGHEST


def passed_along(value, axis, steps):
    count = lax.axis_size(axis)
    first, last = (max(0, -steps), min(count, count - steps))
    return lax.ppermute(value, axis, [(source, source + steps) for source in range(first, last)])


def product(factor_a, factor_b):
    return jnp.dot(factor_a, factor_b, precision=highest, preferred_element_type=jnp.float32)


def left_apply(matrix_re, matrix_im, value_re, value_im):
    columns = value_re.shape[1]
    joined = jnp.concatenate([value_re, value_im], axis=1)
    product_one = product(matrix_re, joined)
    second = product(matrix_im, joined)
    return (
        product_one[:, :columns] - second[:, columns:],
        product_one[:, columns:] + second[:, :columns],
    )


def right_apply(value_re, value_im, matrix_re, matrix_im):
    height = value_re.shape[0]
    joined = jnp.concatenate([value_re, value_im], axis=0)
    product_one = product(joined, matrix_re)
    second = product(joined, matrix_im)
    return (product_one[:height] - second[height:], second[:height] + product_one[height:])


def sandwich(matrix_re, matrix_im, value_re, value_im):
    middle_re, middle_im = left_apply(matrix_re, matrix_im, value_re, value_im)
    return right_apply(middle_re, middle_im, matrix_re, matrix_im)


def tables(extent):
    indices = jnp.arange(extent, dtype=jnp.int32)
    products = indices[:, None] * indices[None, :] % extent
    angles = -2.0 * math.pi / extent * products.astype(jnp.float32)
    norming = 1.0 / math.sqrt(extent)
    dft_re = jnp.cos(angles) * norming
    dft_im = jnp.sin(angles) * norming
    signed = (
        jnp.where(indices < (extent + 1) // 2, indices, indices - extent).astype(jnp.float32)
        / extent
    )
    phases = -fresnel_phase * signed * signed
    line_re = jnp.cos(phases)
    line_im = jnp.sin(phases)
    scaled_re = line_re[:, None] * dft_re - line_im[:, None] * dft_im
    scaled_im = line_re[:, None] * dft_im + line_im[:, None] * dft_re
    fresnel_re, fresnel_im = left_apply(dft_re, -dft_im, scaled_re, scaled_im)
    return (dft_re, dft_im, fresnel_re, fresnel_im)


def pass_down(outgoing):
    return passed_along(outgoing, "cuts", 1)


def pass_up(outgoing):
    return passed_along(outgoing, "cuts", -1)


def on_device(object_slices, probe, intensities, offsets):
    obj_re = object_slices[0, 0]
    obj_im = object_slices[1, 0]
    extent = probe.shape[1]
    positions = offsets.shape[0]
    sections = lax.axis_size("cuts")
    section_index = lax.axis_index("cuts")
    is_last = section_index == sections - 1
    dft_re, dft_im, fresnel_re, fresnel_im = tables(extent)
    blank_wave = jnp.zeros((2, extent, extent), jnp.bfloat16)

    def corner_of(slot_index):
        return (offsets[slot_index, 0], offsets[slot_index, 1])

    def window(source, slot_index):
        return lax.dynamic_slice(source, corner_of(slot_index), (extent, extent))

    def accumulate(running, contrib, slot_index):
        corner = corner_of(slot_index)
        return lax.dynamic_update_slice(
            running, lax.dynamic_slice(running, corner, (extent, extent)) + contrib, corner
        )

    def settle(grad_re, grad_im, slot_index, stored, totals):
        wave_f = stored[slot_index].astype(jnp.float32)
        piece_re = window(obj_re, slot_index)
        piece_im = window(obj_im, slot_index)
        contrib_re = wave_f[0] * grad_re + wave_f[1] * grad_im
        contrib_im = wave_f[0] * grad_im - wave_f[1] * grad_re
        bright = wave_f[0] * wave_f[0] + wave_f[1] * wave_f[1]
        totals = (
            accumulate(totals[0], contrib_re, slot_index),
            accumulate(totals[1], contrib_im, slot_index),
            accumulate(totals[2], bright, slot_index),
        )
        sent_back = jnp.stack(
            [piece_re * grad_re + piece_im * grad_im, piece_re * grad_im - piece_im * grad_re]
        ).astype(jnp.bfloat16)
        return (sent_back, totals)

    def forward(wave_in, slot_index, stored, totals):
        stored = lax.dynamic_update_index_in_dim(stored, wave_in, slot_index, 0)
        wave_re = wave_in[0].astype(jnp.float32)
        wave_im = wave_in[1].astype(jnp.float32)
        piece_re = window(obj_re, slot_index)
        piece_im = window(obj_im, slot_index)
        trans_re = piece_re * wave_re - piece_im * wave_im
        trans_im = piece_re * wave_im + piece_im * wave_re

        def middle():
            next_re, next_im = sandwich(fresnel_re, fresnel_im, trans_re, trans_im)
            return (jnp.stack([next_re, next_im]).astype(jnp.bfloat16), blank_wave, totals)

        def final():
            far_re, far_im = sandwich(dft_re, dft_im, trans_re, trans_im)
            misfit = far_re * far_re + far_im * far_im - intensities[slot_index]
            grad_re, grad_im = sandwich(dft_re, -dft_im, misfit * far_re, misfit * far_im)
            sent_back, new_totals = settle(grad_re, grad_im, slot_index, stored, totals)
            return (blank_wave, sent_back, new_totals)

        downward, upward, totals = lax.cond(is_last, final, middle)
        return (downward, upward, stored, totals)

    def backward(arrived, slot_index, stored, totals):
        grad_re, grad_im = sandwich(
            fresnel_re, -fresnel_im, arrived[0].astype(jnp.float32), arrived[1].astype(jnp.float32)
        )
        return settle(grad_re, grad_im, slot_index, stored, totals)

    def position(raw_slot):
        return ((raw_slot >= 0) & (raw_slot < positions), jnp.clip(raw_slot, 0, positions - 1))

    blank_field = jnp.zeros_like(obj_re)
    totals = (blank_field, blank_field, blank_field)
    stored = jnp.zeros((positions, 2, extent, extent), jnp.bfloat16)

    def forward_turn(step_index, carried):
        arrived, stored, outgoing, totals = carried
        active, slot_index = position(step_index - section_index)
        wave_in = jnp.where(section_index == 0, probe, arrived)

        def advance():
            downward, upward, new_stored, new_totals = forward(wave_in, slot_index, stored, totals)
            return (
                downward,
                lax.dynamic_update_index_in_dim(outgoing, upward, slot_index, 0),
                new_stored,
                new_totals,
            )

        def forward_skipped():
            return (blank_wave, outgoing, stored, totals)

        downward, outgoing, stored, totals = lax.cond(active, advance, forward_skipped)
        return (pass_down(downward), stored, outgoing, totals)

    carried = lax.fori_loop(
        0, sections + positions - 1, forward_turn, (blank_wave, stored, stored, totals)
    )
    stored = carried[1]
    outgoing = carried[2]
    totals = carried[3]

    def backward_turn(step_index, carried):
        arrived, totals = carried
        active, slot_index = position(step_index - (sections - 1 - section_index))

        def release():
            return (outgoing[slot_index], totals)

        def compute():
            return backward(arrived, slot_index, stored, totals)

        def backward_skipped():
            return (blank_wave, totals)

        upward, totals = lax.cond(
            active, lambda: lax.cond(is_last, release, compute), backward_skipped
        )
        return (pass_up(upward), totals)

    carried = lax.fori_loop(0, sections + positions - 1, backward_turn, (blank_wave, totals))
    totals = carried[1]
    summed = (
        lax.psum(totals[0].astype(jnp.bfloat16), "probe").astype(jnp.float32),
        lax.psum(totals[1].astype(jnp.bfloat16), "probe").astype(jnp.float32),
        lax.psum(totals[2].astype(jnp.bfloat16), "probe").astype(jnp.float32),
    )
    factor = step_size / (summed[2] + regular)
    updated = jnp.stack([obj_re - factor * summed[0], obj_im - factor * summed[1]])
    return updated[:, None]


def solution(mesh):
    in_specs = (
        P(None, ("group", "cuts"), None, None),
        P("group", None, None),
        P(("group", "probe"), None, None),
        P(("group", "probe"), None),
    )
    out_specs = P(None, ("group", "cuts"), None, None)
    return jax.shard_map(
        on_device, mesh=mesh, in_specs=in_specs, out_specs=out_specs, check_vma=False
    )
```

profile of v0, /device:TPU:0, one launch (start us, length us, event | category | flops | bytes accessed | tf_op | source)
XLA Modules:
  0.0 518.9 jit_solution(13163026072565088134)
XLA Ops:
  12.4 224.0 %while.48 = (s32[]{:T(128)}, bf16[2,128,128]{2,1,0:T(8,128)(2,1)S(1)}, bf16[8,2,128,128]{3,2,1,0:T(8,128)(2,1)}, bf16[8,2,128,128]{3,2,1,0:T(8,128)(2,1)}, f32[3...) while((s32[]{:T(128)}, ...), condition=%wide.region_5.6_spmd.clone.clone, body=%wide.region_0.5_spmd.clone.clone.sunk | while | flops 403931136 | bytes 7801372 | solution.py:172
  12.4 8.7 %conditional.10 = (bf16[2,128,128]{2,1,0:T(8,128)(2,1)}, bf16[8,2,128,128]{3,2,1,0:T(8,128)(2,1)}, bf16[8,2,128,128]{3,2,1,0:T(8,128)(2,1)}, f32[384,384]{1,0:T(...) conditional(s32[]{:T(128)} %convert_element_type.184, (bf16[8,2,128,128]{3,2,1,0:T(8,128)(2,1)}, ...), branch_computations={%region_1.1_spmd, %region_2.4_spmd.clone} | conditional | flops 403701760 | bytes 7407685 | solution.py:169
  53.9 8.7 %conditional.10 = (bf16[2,128,128]{2,1,0:T(8,128)(2,1)}, bf16[8,2,128,128]{3,2,1,0:T(8,128)(2,1)}, bf16[8,2,128,128]{3,2,1,0:T(8,128)(2,1)}, f32[384,384]{1,0:T(...) conditional(s32[]{:T(128)} %convert_element_type.184, (bf16[8,2,128,128]{3,2,1,0:T(8,128)(2,1)}, ...), branch_computations={%region_1.1_spmd, %region_2.4_spmd.clone} | conditional | flops 403701760 | bytes 7407685 | solution.py:169
  68.2 8.7 %conditional.10 = (bf16[2,128,128]{2,1,0:T(8,128)(2,1)}, bf16[8,2,128,128]{3,2,1,0:T(8,128)(2,1)}, bf16[8,2,128,128]{3,2,1,0:T(8,128)(2,1)}, f32[384,384]{1,0:T(...) conditional(s32[]{:T(128)} %convert_element_type.184, (bf16[8,2,128,128]{3,2,1,0:T(8,128)(2,1)}, ...), branch_computations={%region_1.1_spmd, %region_2.4_spmd.clone} | conditional | flops 403701760 | bytes 7407685 | solution.py:169
  82.5 8.7 %conditional.10 = (bf16[2,128,128]{2,1,0:T(8,128)(2,1)}, bf16[8,2,128,128]{3,2,1,0:T(8,128)(2,1)}, bf16[8,2,128,128]{3,2,1,0:T(8,128)(2,1)}, f32[384,384]{1,0:T(...) conditional(s32[]{:T(128)} %convert_element_type.184, (bf16[8,2,128,128]{3,2,1,0:T(8,128)(2,1)}, ...), branch_computations={%region_1.1_spmd, %region_2.4_spmd.clone} | conditional | flops 403701760 | bytes 7407685 | solution.py:169
  91.3 11.4 %collective-permute-start.1 = (bf16[2,128,128]{2,1,0:T(8,128)(2,1)}, bf16[2,128,128]{2,1,0:T(8,128)(2,1)S(1)}, u32[]{:S(2)}, u32[]{:S(2)}) collective-permute-start(bf16[2,128,128]{2,1,0:T(8,128)(2,1)} %get-tuple-element.1571), channel_id=1, source_target_pairs={{0,4},{4,8},{8,12},{1,5},{5,9},{9,13},{2,6},{6,10},{10,14},{3,7},{... | collective-permute-start | bytes 196616 | tf_op jit(solution)/shard_map/while/body/eval_jaxpr/ppermute | solution.py:17
  113.7 16.9 %collective-permute-start.1 = (bf16[2,128,128]{2,1,0:T(8,128)(2,1)}, bf16[2,128,128]{2,1,0:T(8,128)(2,1)S(1)}, u32[]{:S(2)}, u32[]{:S(2)}) collective-permute-start(bf16[2,128,128]{2,1,0:T(8,128)(2,1)} %get-tuple-element.1571), channel_id=1, source_target_pairs={{0,4},{4,8},{8,12},{1,5},{5,9},{9,13},{2,6},{6,10},{10,14},{3,7},{... | collective-permute-start | bytes 196616 | tf_op jit(solution)/shard_map/while/body/eval_jaxpr/ppermute | solution.py:17
  141.6 17.0 %collective-permute-start.1 = (bf16[2,128,128]{2,1,0:T(8,128)(2,1)}, bf16[2,128,128]{2,1,0:T(8,128)(2,1)S(1)}, u32[]{:S(2)}, u32[]{:S(2)}) collective-permute-start(bf16[2,128,128]{2,1,0:T(8,128)(2,1)} %get-tuple-element.1571), channel_id=1, source_target_pairs={{0,4},{4,8},{8,12},{1,5},{5,9},{9,13},{2,6},{6,10},{10,14},{3,7},{... | collective-permute-start | bytes 196616 | tf_op jit(solution)/shard_map/while/body/eval_jaxpr/ppermute | solution.py:17
  161.6 25.0 %collective-permute-start.1 = (bf16[2,128,128]{2,1,0:T(8,128)(2,1)}, bf16[2,128,128]{2,1,0:T(8,128)(2,1)S(1)}, u32[]{:S(2)}, u32[]{:S(2)}) collective-permute-start(bf16[2,128,128]{2,1,0:T(8,128)(2,1)} %get-tuple-element.1571), channel_id=1, source_target_pairs={{0,4},{4,8},{8,12},{1,5},{5,9},{9,13},{2,6},{6,10},{10,14},{3,7},{... | collective-permute-start | bytes 196616 | tf_op jit(solution)/shard_map/while/body/eval_jaxpr/ppermute | solution.py:17
  189.5 17.8 %collective-permute-start.1 = (bf16[2,128,128]{2,1,0:T(8,128)(2,1)}, bf16[2,128,128]{2,1,0:T(8,128)(2,1)S(1)}, u32[]{:S(2)}, u32[]{:S(2)}) collective-permute-start(bf16[2,128,128]{2,1,0:T(8,128)(2,1)} %get-tuple-element.1571), channel_id=1, source_target_pairs={{0,4},{4,8},{8,12},{1,5},{5,9},{9,13},{2,6},{6,10},{10,14},{3,7},{... | collective-permute-start | bytes 196616 | tf_op jit(solution)/shard_map/while/body/eval_jaxpr/ppermute | solution.py:17
  210.3 23.9 %collective-permute-start.1 = (bf16[2,128,128]{2,1,0:T(8,128)(2,1)}, bf16[2,128,128]{2,1,0:T(8,128)(2,1)S(1)}, u32[]{:S(2)}, u32[]{:S(2)}) collective-permute-start(bf16[2,128,128]{2,1,0:T(8,128)(2,1)} %get-tuple-element.1571), channel_id=1, source_target_pairs={{0,4},{4,8},{8,12},{1,5},{5,9},{9,13},{2,6},{6,10},{10,14},{3,7},{... | collective-permute-start | bytes 196616 | tf_op jit(solution)/shard_map/while/body/eval_jaxpr/ppermute | solution.py:17
  236.4 234.5 %while.47 = (s32[]{:T(128)}, bf16[2,128,128]{2,1,0:T(8,128)(2,1)S(1)}, f32[384,384]{1,0:T(8,128)S(1)}, f32[384,384]{1,0:T(8,128)S(1)}, f32[384,384]{1,0:T(8,128)...) while((s32[]{:T(128)}, ...), condition=%wide.region_11.12_spmd, body=%wide.region_6.11_spmd.sunk | while | flops 202145792 | bytes 4063946 | solution.py:197
  238.3 19.0 %collective-permute-done = bf16[2,128,128]{2,1,0:T(8,128)(2,1)S(1)} collective-permute-done((bf16[2,128,128]{2,1,0:T(8,128)(2,1)}, bf16[2,128,128]{2,1,0:T(8,128)(2,1)S(1)}, u32[]{:S(2)}, u32[]{:S(2)}) %collective-permute-start) | collective-permute-done | bytes 65568 | tf_op jit(solution)/shard_map/while/body/eval_jaxpr/ppermute | solution.py:17
  259.2 25.2 %collective-permute-done = bf16[2,128,128]{2,1,0:T(8,128)(2,1)S(1)} collective-permute-done((bf16[2,128,128]{2,1,0:T(8,128)(2,1)}, bf16[2,128,128]{2,1,0:T(8,128)(2,1)S(1)}, u32[]{:S(2)}, u32[]{:S(2)}) %collective-permute-start) | collective-permute-done | bytes 65568 | tf_op jit(solution)/shard_map/while/body/eval_jaxpr/ppermute | solution.py:17
  286.3 28.5 %collective-permute-done = bf16[2,128,128]{2,1,0:T(8,128)(2,1)S(1)} collective-permute-done((bf16[2,128,128]{2,1,0:T(8,128)(2,1)}, bf16[2,128,128]{2,1,0:T(8,128)(2,1)S(1)}, u32[]{:S(2)}, u32[]{:S(2)}) %collective-permute-start) | collective-permute-done | bytes 65568 | tf_op jit(solution)/shard_map/while/body/eval_jaxpr/ppermute | solution.py:17
  314.9 12.1 %conditional.9 = ((bf16[2,128,128]{2,1,0:T(8,128)(2,1)}, f32[384,384]{1,0:T(8,128)S(1)}, f32[384,384]{1,0:T(8,128)S(1)}, f32[384,384]{1,0:T(8,128)S(1)})) conditional(s32[]{:T(128)} %convert_element_type.182, (f32[384,384]{1,0:T(8,128)S(1)}, f32[384,384]{1,0:T(8,128)S(1)}, f32[384,384]{1,0:T(8,128)S(1)}) %tuple.153, (pred[]{:T(512)}, s32[]{:T(128)}, ...), branch_computations={%region_7.7_spmd, %region_8.10_spmd} | conditional | flops 202145792 | bytes 3801439 | solution.py:192
  314.9 12.1 %conditional.2 = (bf16[2,128,128]{2,1,0:T(8,128)(2,1)}, f32[384,384]{1,0:T(8,128)S(1)}, f32[384,384]{1,0:T(8,128)S(1)}, f32[384,384]{1,0:T(8,128)S(1)}) conditional(s32[]{:T(128)} %convert_element_type.96, (s32[]{:T(128)}, s32[8,2]{0,1:T(2,128)S(1)}, f32[384,384]{1,0:T(8,128)S(1)}, bf16[2,128,128]{2,1,0:T(8,128)(2,1)S(1)}, f32[128,128]{1,0:T(8,128)S(1)}, ...), branch_computations={%region_9.8_spmd, %region_10.9_spmd} | conditional | flops 202145792 | bytes 3801274 | solution.py:193
  335.6 13.2 %conditional.9 = ((bf16[2,128,128]{2,1,0:T(8,128)(2,1)}, f32[384,384]{1,0:T(8,128)S(1)}, f32[384,384]{1,0:T(8,128)S(1)}, f32[384,384]{1,0:T(8,128)S(1)})) conditional(s32[]{:T(128)} %convert_element_type.182, (f32[384,384]{1,0:T(8,128)S(1)}, f32[384,384]{1,0:T(8,128)S(1)}, f32[384,384]{1,0:T(8,128)S(1)}) %tuple.153, (pred[]{:T(512)}, s32[]{:T(128)}, ...), branch_computations={%region_7.7_spmd, %region_8.10_spmd} | conditional | flops 202145792 | bytes 3801439 | solution.py:192
  335.6 13.2 %conditional.2 = (bf16[2,128,128]{2,1,0:T(8,128)(2,1)}, f32[384,384]{1,0:T(8,128)S(1)}, f32[384,384]{1,0:T(8,128)S(1)}, f32[384,384]{1,0:T(8,128)S(1)}) conditional(s32[]{:T(128)} %convert_element_type.96, (s32[]{:T(128)}, s32[8,2]{0,1:T(2,128)S(1)}, f32[384,384]{1,0:T(8,128)S(1)}, bf16[2,128,128]{2,1,0:T(8,128)(2,1)S(1)}, f32[128,128]{1,0:T(8,128)S(1)}, ...), branch_computations={%region_9.8_spmd, %region_10.9_spmd} | conditional | flops 202145792 | bytes 3801274 | solution.py:193
  355.2 13.2 %conditional.9 = ((bf16[2,128,128]{2,1,0:T(8,128)(2,1)}, f32[384,384]{1,0:T(8,128)S(1)}, f32[384,384]{1,0:T(8,128)S(1)}, f32[384,384]{1,0:T(8,128)S(1)})) conditional(s32[]{:T(128)} %convert_element_type.182, (f32[384,384]{1,0:T(8,128)S(1)}, f32[384,384]{1,0:T(8,128)S(1)}, f32[384,384]{1,0:T(8,128)S(1)}) %tuple.153, (pred[]{:T(512)}, s32[]{:T(128)}, ...), branch_computations={%region_7.7_spmd, %region_8.10_spmd} | conditional | flops 202145792 | bytes 3801439 | solution.py:192
  355.2 13.2 %conditional.2 = (bf16[2,128,128]{2,1,0:T(8,128)(2,1)}, f32[384,384]{1,0:T(8,128)S(1)}, f32[384,384]{1,0:T(8,128)S(1)}, f32[384,384]{1,0:T(8,128)S(1)}) conditional(s32[]{:T(128)} %convert_element_type.96, (s32[]{:T(128)}, s32[8,2]{0,1:T(2,128)S(1)}, f32[384,384]{1,0:T(8,128)S(1)}, bf16[2,128,128]{2,1,0:T(8,128)(2,1)S(1)}, f32[128,128]{1,0:T(8,128)S(1)}, ...), branch_computations={%region_9.8_spmd, %region_10.9_spmd} | conditional | flops 202145792 | bytes 3801274 | solution.py:193
  374.8 13.2 %conditional.9 = ((bf16[2,128,128]{2,1,0:T(8,128)(2,1)}, f32[384,384]{1,0:T(8,128)S(1)}, f32[384,384]{1,0:T(8,128)S(1)}, f32[384,384]{1,0:T(8,128)S(1)})) conditional(s32[]{:T(128)} %convert_element_type.182, (f32[384,384]{1,0:T(8,128)S(1)}, f32[384,384]{1,0:T(8,128)S(1)}, f32[384,384]{1,0:T(8,128)S(1)}) %tuple.153, (pred[]{:T(512)}, s32[]{:T(128)}, ...), branch_computations={%region_7.7_spmd, %region_8.10_spmd} | conditional | flops 202145792 | bytes 3801439 | solution.py:192
  374.8 13.2 %conditional.2 = (bf16[2,128,128]{2,1,0:T(8,128)(2,1)}, f32[384,384]{1,0:T(8,128)S(1)}, f32[384,384]{1,0:T(8,128)S(1)}, f32[384,384]{1,0:T(8,128)S(1)}) conditional(s32[]{:T(128)} %convert_element_type.96, (s32[]{:T(128)}, s32[8,2]{0,1:T(2,128)S(1)}, f32[384,384]{1,0:T(8,128)S(1)}, bf16[2,128,128]{2,1,0:T(8,128)(2,1)S(1)}, f32[128,128]{1,0:T(8,128)S(1)}, ...), branch_computations={%region_9.8_spmd, %region_10.9_spmd} | conditional | flops 202145792 | bytes 3801274 | solution.py:193
  394.7 13.2 %conditional.9 = ((bf16[2,128,128]{2,1,0:T(8,128)(2,1)}, f32[384,384]{1,0:T(8,128)S(1)}, f32[384,384]{1,0:T(8,128)S(1)}, f32[384,384]{1,0:T(8,128)S(1)})) conditional(s32[]{:T(128)} %convert_element_type.182, (f32[384,384]{1,0:T(8,128)S(1)}, f32[384,384]{1,0:T(8,128)S(1)}, f32[384,384]{1,0:T(8,128)S(1)}) %tuple.153, (pred[]{:T(512)}, s32[]{:T(128)}, ...), branch_computations={%region_7.7_spmd, %region_8.10_spmd} | conditional | flops 202145792 | bytes 3801439 | solution.py:192
  394.7 13.2 %conditional.2 = (bf16[2,128,128]{2,1,0:T(8,128)(2,1)}, f32[384,384]{1,0:T(8,128)S(1)}, f32[384,384]{1,0:T(8,128)S(1)}, f32[384,384]{1,0:T(8,128)S(1)}) conditional(s32[]{:T(128)} %convert_element_type.96, (s32[]{:T(128)}, s32[8,2]{0,1:T(2,128)S(1)}, f32[384,384]{1,0:T(8,128)S(1)}, bf16[2,128,128]{2,1,0:T(8,128)(2,1)S(1)}, f32[128,128]{1,0:T(8,128)S(1)}, ...), branch_computations={%region_9.8_spmd, %region_10.9_spmd} | conditional | flops 202145792 | bytes 3801274 | solution.py:193
  414.3 12.1 %conditional.9 = ((bf16[2,128,128]{2,1,0:T(8,128)(2,1)}, f32[384,384]{1,0:T(8,128)S(1)}, f32[384,384]{1,0:T(8,128)S(1)}, f32[384,384]{1,0:T(8,128)S(1)})) conditional(s32[]{:T(128)} %convert_element_type.182, (f32[384,384]{1,0:T(8,128)S(1)}, f32[384,384]{1,0:T(8,128)S(1)}, f32[384,384]{1,0:T(8,128)S(1)}) %tuple.153, (pred[]{:T(512)}, s32[]{:T(128)}, ...), branch_computations={%region_7.7_spmd, %region_8.10_spmd} | conditional | flops 202145792 | bytes 3801439 | solution.py:192
  414.3 12.1 %conditional.2 = (bf16[2,128,128]{2,1,0:T(8,128)(2,1)}, f32[384,384]{1,0:T(8,128)S(1)}, f32[384,384]{1,0:T(8,128)S(1)}, f32[384,384]{1,0:T(8,128)S(1)}) conditional(s32[]{:T(128)} %convert_element_type.96, (s32[]{:T(128)}, s32[8,2]{0,1:T(2,128)S(1)}, f32[384,384]{1,0:T(8,128)S(1)}, bf16[2,128,128]{2,1,0:T(8,128)(2,1)S(1)}, f32[128,128]{1,0:T(8,128)S(1)}, ...), branch_computations={%region_9.8_spmd, %region_10.9_spmd} | conditional | flops 202145792 | bytes 3801274 | solution.py:193
  432.7 13.2 %conditional.9 = ((bf16[2,128,128]{2,1,0:T(8,128)(2,1)}, f32[384,384]{1,0:T(8,128)S(1)}, f32[384,384]{1,0:T(8,128)S(1)}, f32[384,384]{1,0:T(8,128)S(1)})) conditional(s32[]{:T(128)} %convert_element_type.182, (f32[384,384]{1,0:T(8,128)S(1)}, f32[384,384]{1,0:T(8,128)S(1)}, f32[384,384]{1,0:T(8,128)S(1)}) %tuple.153, (pred[]{:T(512)}, s32[]{:T(128)}, ...), branch_computations={%region_7.7_spmd, %region_8.10_spmd} | conditional | flops 202145792 | bytes 3801439 | solution.py:192
  432.7 13.2 %conditional.2 = (bf16[2,128,128]{2,1,0:T(8,128)(2,1)}, f32[384,384]{1,0:T(8,128)S(1)}, f32[384,384]{1,0:T(8,128)S(1)}, f32[384,384]{1,0:T(8,128)S(1)}) conditional(s32[]{:T(128)} %convert_element_type.96, (s32[]{:T(128)}, s32[8,2]{0,1:T(2,128)S(1)}, f32[384,384]{1,0:T(8,128)S(1)}, bf16[2,128,128]{2,1,0:T(8,128)(2,1)S(1)}, f32[128,128]{1,0:T(8,128)S(1)}, ...), branch_computations={%region_9.8_spmd, %region_10.9_spmd} | conditional | flops 202145792 | bytes 3801274 | solution.py:193
  452.3 12.2 %conditional.9 = ((bf16[2,128,128]{2,1,0:T(8,128)(2,1)}, f32[384,384]{1,0:T(8,128)S(1)}, f32[384,384]{1,0:T(8,128)S(1)}, f32[384,384]{1,0:T(8,128)S(1)})) conditional(s32[]{:T(128)} %convert_element_type.182, (f32[384,384]{1,0:T(8,128)S(1)}, f32[384,384]{1,0:T(8,128)S(1)}, f32[384,384]{1,0:T(8,128)S(1)}) %tuple.153, (pred[]{:T(512)}, s32[]{:T(128)}, ...), branch_computations={%region_7.7_spmd, %region_8.10_spmd} | conditional | flops 202145792 | bytes 3801439 | solution.py:192
  452.3 12.2 %conditional.2 = (bf16[2,128,128]{2,1,0:T(8,128)(2,1)}, f32[384,384]{1,0:T(8,128)S(1)}, f32[384,384]{1,0:T(8,128)S(1)}, f32[384,384]{1,0:T(8,128)S(1)}) conditional(s32[]{:T(128)} %convert_element_type.96, (s32[]{:T(128)}, s32[8,2]{0,1:T(2,128)S(1)}, f32[384,384]{1,0:T(8,128)S(1)}, bf16[2,128,128]{2,1,0:T(8,128)(2,1)S(1)}, f32[128,128]{1,0:T(8,128)S(1)}, ...), branch_computations={%region_9.8_spmd, %region_10.9_spmd} | conditional | flops 202145792 | bytes 3801274 | solution.py:193
  473.1 36.5 %all-reduce.3.cloned.1.call-done = (bf16[384,384]{1,0:T(8,128)(2,1)}, bf16[384,384]{1,0:T(8,128)(2,1)}, bf16[384,384]{1,0:T(8,128)(2,1)}) async-done(((bf16[384,384]{1,0:T(8,128)(2,1)}, bf16[384,384]{1,0:T(8,128)(2,1)}, bf16[384,384]{1,0:T(8,128)(2,1)}), (bf16[384,384]{1,0:T(8,128)(2,1)}, bf16[384,384]{1,0:T(8,128)(2,1)}, bf16[384,384]{1,0:T(8,128)(2,1)})) %all-reduce.3.cloned.1.call-update) | async-done | bytes 884752 | tf_op jit(solution)/shard_map/psum | solution.py:201
  (340 shorter events, 277.7 us)
Async XLA Ops:
  6.5 503.1 %all-reduce.3.cloned.1.call-start = ((), (), s32[]{:S(2)}) async-start(), calls=%async_computation | async-start | bytes 1769472 | tf_op jit(solution)/shard_map/psum | solution.py:201
  7.9 1.4 copy-start.1
  10.4 2.0 copy-start.2
  21.2 3.8 collective-permute-start.1
  33.8 5.7 %collective-permute-start.1 = (bf16[2,128,128]{2,1,0:T(8,128)(2,1)}, bf16[2,128,128]{2,1,0:T(8,128)(2,1)S(1)}, u32[]{:S(2)}, u32[]{:S(2)}) collective-permute-start(bf16[2,128,128]{2,1,0:T(8,128)(2,1)} %get-tuple-element.1571), channel_id=1, source_target_pairs={{0,4},{4,8},{8,12},{1,5},{5,9},{9,13},{2,6},{6,10},{10,14},{3,7},{... | collective-permute-start | bytes 196616 | tf_op jit(solution)/shard_map/while/body/eval_jaxpr/ppermute | solution.py:17
  48.3 5.5 %collective-permute-start.1 = (bf16[2,128,128]{2,1,0:T(8,128)(2,1)}, bf16[2,128,128]{2,1,0:T(8,128)(2,1)S(1)}, u32[]{:S(2)}, u32[]{:S(2)}) collective-permute-start(bf16[2,128,128]{2,1,0:T(8,128)(2,1)} %get-tuple-element.1571), channel_id=1, source_target_pairs={{0,4},{4,8},{8,12},{1,5},{5,9},{9,13},{2,6},{6,10},{10,14},{3,7},{... | collective-permute-start | bytes 196616 | tf_op jit(solution)/shard_map/while/body/eval_jaxpr/ppermute | solution.py:17
  62.6 5.5 %collective-permute-start.1 = (bf16[2,128,128]{2,1,0:T(8,128)(2,1)}, bf16[2,128,128]{2,1,0:T(8,128)(2,1)S(1)}, u32[]{:S(2)}, u32[]{:S(2)}) collective-permute-start(bf16[2,128,128]{2,1,0:T(8,128)(2,1)} %get-tuple-element.1571), channel_id=1, source_target_pairs={{0,4},{4,8},{8,12},{1,5},{5,9},{9,13},{2,6},{6,10},{10,14},{3,7},{... | collective-permute-start | bytes 196616 | tf_op jit(solution)/shard_map/while/body/eval_jaxpr/ppermute | solution.py:17
  76.9 5.5 %collective-permute-start.1 = (bf16[2,128,128]{2,1,0:T(8,128)(2,1)}, bf16[2,128,128]{2,1,0:T(8,128)(2,1)S(1)}, u32[]{:S(2)}, u32[]{:S(2)}) collective-permute-start(bf16[2,128,128]{2,1,0:T(8,128)(2,1)} %get-tuple-element.1571), channel_id=1, source_target_pairs={{0,4},{4,8},{8,12},{1,5},{5,9},{9,13},{2,6},{6,10},{10,14},{3,7},{... | collective-permute-start | bytes 196616 | tf_op jit(solution)/shard_map/while/body/eval_jaxpr/ppermute | solution.py:17
  91.3 13.6 %collective-permute-start.1 = (bf16[2,128,128]{2,1,0:T(8,128)(2,1)}, bf16[2,128,128]{2,1,0:T(8,128)(2,1)S(1)}, u32[]{:S(2)}, u32[]{:S(2)}) collective-permute-start(bf16[2,128,128]{2,1,0:T(8,128)(2,1)} %get-tuple-element.1571), channel_id=1, source_target_pairs={{0,4},{4,8},{8,12},{1,5},{5,9},{9,13},{2,6},{6,10},{10,14},{3,7},{... | collective-permute-start | bytes 196616 | tf_op jit(solution)/shard_map/while/body/eval_jaxpr/ppermute | solution.py:17
  113.7 19.2 %collective-permute-start.1 = (bf16[2,128,128]{2,1,0:T(8,128)(2,1)}, bf16[2,128,128]{2,1,0:T(8,128)(2,1)S(1)}, u32[]{:S(2)}, u32[]{:S(2)}) collective-permute-start(bf16[2,128,128]{2,1,0:T(8,128)(2,1)} %get-tuple-element.1571), channel_id=1, source_target_pairs={{0,4},{4,8},{8,12},{1,5},{5,9},{9,13},{2,6},{6,10},{10,14},{3,7},{... | collective-permute-start | bytes 196616 | tf_op jit(solution)/shard_map/while/body/eval_jaxpr/ppermute | solution.py:17
  141.6 19.2 %collective-permute-start.1 = (bf16[2,128,128]{2,1,0:T(8,128)(2,1)}, bf16[2,128,128]{2,1,0:T(8,128)(2,1)S(1)}, u32[]{:S(2)}, u32[]{:S(2)}) collective-permute-start(bf16[2,128,128]{2,1,0:T(8,128)(2,1)} %get-tuple-element.1571), channel_id=1, source_target_pairs={{0,4},{4,8},{8,12},{1,5},{5,9},{9,13},{2,6},{6,10},{10,14},{3,7},{... | collective-permute-start | bytes 196616 | tf_op jit(solution)/shard_map/while/body/eval_jaxpr/ppermute | solution.py:17
  161.6 27.3 %collective-permute-start.1 = (bf16[2,128,128]{2,1,0:T(8,128)(2,1)}, bf16[2,128,128]{2,1,0:T(8,128)(2,1)S(1)}, u32[]{:S(2)}, u32[]{:S(2)}) collective-permute-start(bf16[2,128,128]{2,1,0:T(8,128)(2,1)} %get-tuple-element.1571), channel_id=1, source_target_pairs={{0,4},{4,8},{8,12},{1,5},{5,9},{9,13},{2,6},{6,10},{10,14},{3,7},{... | collective-permute-start | bytes 196616 | tf_op jit(solution)/shard_map/while/body/eval_jaxpr/ppermute | solution.py:17
  189.5 20.0 %collective-permute-start.1 = (bf16[2,128,128]{2,1,0:T(8,128)(2,1)}, bf16[2,128,128]{2,1,0:T(8,128)(2,1)S(1)}, u32[]{:S(2)}, u32[]{:S(2)}) collective-permute-start(bf16[2,128,128]{2,1,0:T(8,128)(2,1)} %get-tuple-element.1571), channel_id=1, source_target_pairs={{0,4},{4,8},{8,12},{1,5},{5,9},{9,13},{2,6},{6,10},{10,14},{3,7},{... | collective-permute-start | bytes 196616 | tf_op jit(solution)/shard_map/while/body/eval_jaxpr/ppermute | solution.py:17
  210.3 26.1 %collective-permute-start.1 = (bf16[2,128,128]{2,1,0:T(8,128)(2,1)}, bf16[2,128,128]{2,1,0:T(8,128)(2,1)S(1)}, u32[]{:S(2)}, u32[]{:S(2)}) collective-permute-start(bf16[2,128,128]{2,1,0:T(8,128)(2,1)} %get-tuple-element.1571), channel_id=1, source_target_pairs={{0,4},{4,8},{8,12},{1,5},{5,9},{9,13},{2,6},{6,10},{10,14},{3,7},{... | collective-permute-start | bytes 196616 | tf_op jit(solution)/shard_map/while/body/eval_jaxpr/ppermute | solution.py:17
  237.0 20.3 %collective-permute-start = (bf16[2,128,128]{2,1,0:T(8,128)(2,1)}, bf16[2,128,128]{2,1,0:T(8,128)(2,1)S(1)}, u32[]{:S(2)}, u32[]{:S(2)}) collective-permute-start(bf16[2,128,128]{2,1,0:T(8,128)(2,1)} %get-tuple-element.1550), channel_id=1, source_target_pairs={{4,0},{8,4},{12,8},{5,1},{9,5},{13,9},{6,2},{10,6},{14,10},{7,3},{... | collective-permute-start | bytes 196616 | tf_op jit(solution)/shard_map/while/body/eval_jaxpr/ppermute | solution.py:17
  257.9 26.5 %collective-permute-start = (bf16[2,128,128]{2,1,0:T(8,128)(2,1)}, bf16[2,128,128]{2,1,0:T(8,128)(2,1)S(1)}, u32[]{:S(2)}, u32[]{:S(2)}) collective-permute-start(bf16[2,128,128]{2,1,0:T(8,128)(2,1)} %get-tuple-element.1550), channel_id=1, source_target_pairs={{4,0},{8,4},{12,8},{5,1},{9,5},{13,9},{6,2},{10,6},{14,10},{7,3},{... | collective-permute-start | bytes 196616 | tf_op jit(solution)/shard_map/while/body/eval_jaxpr/ppermute | solution.py:17
  285.0 29.8 %collective-permute-start = (bf16[2,128,128]{2,1,0:T(8,128)(2,1)}, bf16[2,128,128]{2,1,0:T(8,128)(2,1)S(1)}, u32[]{:S(2)}, u32[]{:S(2)}) collective-permute-start(bf16[2,128,128]{2,1,0:T(8,128)(2,1)} %get-tuple-element.1550), channel_id=1, source_target_pairs={{4,0},{8,4},{12,8},{5,1},{9,5},{13,9},{6,2},{10,6},{14,10},{7,3},{... | collective-permute-start | bytes 196616 | tf_op jit(solution)/shard_map/while/body/eval_jaxpr/ppermute | solution.py:17
  327.0 8.6 %collective-permute-start = (bf16[2,128,128]{2,1,0:T(8,128)(2,1)}, bf16[2,128,128]{2,1,0:T(8,128)(2,1)S(1)}, u32[]{:S(2)}, u32[]{:S(2)}) collective-permute-start(bf16[2,128,128]{2,1,0:T(8,128)(2,1)} %get-tuple-element.1550), channel_id=1, source_target_pairs={{4,0},{8,4},{12,8},{5,1},{9,5},{13,9},{6,2},{10,6},{14,10},{7,3},{... | collective-permute-start | bytes 196616 | tf_op jit(solution)/shard_map/while/body/eval_jaxpr/ppermute | solution.py:17
  348.8 6.4 %collective-permute-start = (bf16[2,128,128]{2,1,0:T(8,128)(2,1)}, bf16[2,128,128]{2,1,0:T(8,128)(2,1)S(1)}, u32[]{:S(2)}, u32[]{:S(2)}) collective-permute-start(bf16[2,128,128]{2,1,0:T(8,128)(2,1)} %get-tuple-element.1550), channel_id=1, source_target_pairs={{4,0},{8,4},{12,8},{5,1},{9,5},{13,9},{6,2},{10,6},{14,10},{7,3},{... | collective-permute-start | bytes 196616 | tf_op jit(solution)/shard_map/while/body/eval_jaxpr/ppermute | solution.py:17
  368.4 6.4 %collective-permute-start = (bf16[2,128,128]{2,1,0:T(8,128)(2,1)}, bf16[2,128,128]{2,1,0:T(8,128)(2,1)S(1)}, u32[]{:S(2)}, u32[]{:S(2)}) collective-permute-start(bf16[2,128,128]{2,1,0:T(8,128)(2,1)} %get-tuple-element.1550), channel_id=1, source_target_pairs={{4,0},{8,4},{12,8},{5,1},{9,5},{13,9},{6,2},{10,6},{14,10},{7,3},{... | collective-permute-start | bytes 196616 | tf_op jit(solution)/shard_map/while/body/eval_jaxpr/ppermute | solution.py:17
  388.0 6.7 %collective-permute-start = (bf16[2,128,128]{2,1,0:T(8,128)(2,1)}, bf16[2,128,128]{2,1,0:T(8,128)(2,1)S(1)}, u32[]{:S(2)}, u32[]{:S(2)}) collective-permute-start(bf16[2,128,128]{2,1,0:T(8,128)(2,1)} %get-tuple-element.1550), channel_id=1, source_target_pairs={{4,0},{8,4},{12,8},{5,1},{9,5},{13,9},{6,2},{10,6},{14,10},{7,3},{... | collective-permute-start | bytes 196616 | tf_op jit(solution)/shard_map/while/body/eval_jaxpr/ppermute | solution.py:17
  407.9 6.4 %collective-permute-start = (bf16[2,128,128]{2,1,0:T(8,128)(2,1)}, bf16[2,128,128]{2,1,0:T(8,128)(2,1)S(1)}, u32[]{:S(2)}, u32[]{:S(2)}) collective-permute-start(bf16[2,128,128]{2,1,0:T(8,128)(2,1)} %get-tuple-element.1550), channel_id=1, source_target_pairs={{4,0},{8,4},{12,8},{5,1},{9,5},{13,9},{6,2},{10,6},{14,10},{7,3},{... | collective-permute-start | bytes 196616 | tf_op jit(solution)/shard_map/while/body/eval_jaxpr/ppermute | solution.py:17
  426.3 6.4 %collective-permute-start = (bf16[2,128,128]{2,1,0:T(8,128)(2,1)}, bf16[2,128,128]{2,1,0:T(8,128)(2,1)S(1)}, u32[]{:S(2)}, u32[]{:S(2)}) collective-permute-start(bf16[2,128,128]{2,1,0:T(8,128)(2,1)} %get-tuple-element.1550), channel_id=1, source_target_pairs={{4,0},{8,4},{12,8},{5,1},{9,5},{13,9},{6,2},{10,6},{14,10},{7,3},{... | collective-permute-start | bytes 196616 | tf_op jit(solution)/shard_map/while/body/eval_jaxpr/ppermute | solution.py:17
  445.9 6.4 %collective-permute-start = (bf16[2,128,128]{2,1,0:T(8,128)(2,1)}, bf16[2,128,128]{2,1,0:T(8,128)(2,1)S(1)}, u32[]{:S(2)}, u32[]{:S(2)}) collective-permute-start(bf16[2,128,128]{2,1,0:T(8,128)(2,1)} %get-tuple-element.1550), channel_id=1, source_target_pairs={{4,0},{8,4},{12,8},{5,1},{9,5},{13,9},{6,2},{10,6},{14,10},{7,3},{... | collective-permute-start | bytes 196616 | tf_op jit(solution)/shard_map/while/body/eval_jaxpr/ppermute | solution.py:17
  464.5 6.4 %collective-permute-start = (bf16[2,128,128]{2,1,0:T(8,128)(2,1)}, bf16[2,128,128]{2,1,0:T(8,128)(2,1)S(1)}, u32[]{:S(2)}, u32[]{:S(2)}) collective-permute-start(bf16[2,128,128]{2,1,0:T(8,128)(2,1)} %get-tuple-element.1550), channel_id=1, source_target_pairs={{4,0},{8,4},{12,8},{5,1},{9,5},{13,9},{6,2},{10,6},{14,10},{7,3},{... | collective-permute-start | bytes 196616 | tf_op jit(solution)/shard_map/while/body/eval_jaxpr/ppermute | solution.py:17
  471.6 38.1 %copy-start = (f32[2,1,384,384]{3,2,1,0:T(8,128)S(1)}, f32[2,1,384,384]{3,2,1,0:T(8,128)}, u32[]{:S(2)}) copy-start(f32[2,1,384,384]{3,2,1,0:T(8,128)} %param.16) | copy-start | bytes 3538948
Sparse Core Ops, SparseCore 0:
  473.2 36.3 all-reduce.2
where the time goes:
time: 523 us; the launch traced here: 519 us
  waiting for transfers between devices  177 us (34%)
  starting transfers between devices  141 us (27%)
  local copies, waits for them, and re-layouts  70.2 us (13%)
  loops' own time  59.9 us (11%)
  other arithmetic  40.8 us (8%)
  matrix products  16.9 us (3%)
  between operations  13.5 us (3%)
    ppermute x22, starting transfers between devices, passed_along(): lax.ppermute(value, axis, [(source, source + steps) for source in range(f...  141 us
    ppermute x22, waiting for transfers between devices, passed_along(): lax.ppermute(value, axis, [(source, source + steps) for source in range(f...  140 us
    dynamic_update_slice x24, local copies, waits for them, and re-layouts, accumulate(): lax.dynamic_update_slice(running, lax.dynamic_slice(running, corner, (ext...  46.4 us
    psum x1, waiting for transfers between devices, on_device(): lax.psum(totals[1].astype(jnp.bfloat16), 'probe').astype(jnp.float32)  36.5 us
    another operation x8, loops' own time, backward_turn(): lax.cond(is_last, release, compute)  29.7 us
    another operation x11, loops' own time, forward_turn(): lax.cond(active, advance, forward_skipped)  28.9 us
    dot_general x66, matrix products, product(): jnp.dot(factor_a, factor_b, precision=highest, preferred_element_type=jnp...  16.9 us
    dynamic_update_slice x8, other arithmetic, forward(): stored = lax.dynamic_update_index_in_dim(stored, wave_in, slot_index, 0)  12 us
  transfers between devices with their start and end apart: 23, of which 23 were waited for; matrix products, arithmetic and copies ran while one was open for 0% of the time, Pallas kernels for 0%

commit v1 on v0

v1 whole, which is shorter than its diff:
```python
import functools
import math

import jax
import jax.numpy as jnp
import ml_dtypes
import numpy as np
from jax import lax
from jax.experimental import pallas as pl
from jax.experimental.pallas import tpu as pltpu
from jax.sharding import PartitionSpec as P

fresnel_phase = 12.0
step_size = 0.5
regular = 1.0
wire = jnp.bfloat16
lanes = 128
resident_bytes = 24 * 2**20


def tables(extent):
    k = np.arange(extent)
    dft = np.exp(-2j * np.pi * (np.outer(k, k) % extent) / extent) / math.sqrt(extent)
    f = np.where(k < (extent + 1) // 2, k, k - extent) / extent
    fresnel = dft.conj() @ (np.exp(-1j * fresnel_phase * f * f)[:, None] * dft)

    def split(matrix):
        high = matrix.astype(ml_dtypes.bfloat16)
        low = (matrix - high.astype(np.float64)).astype(ml_dtypes.bfloat16)
        return high, low

    right, left = [], []
    for matrix in (fresnel, dft):
        real = np.block([[matrix.real, matrix.imag], [-matrix.imag, matrix.real]])
        right.append(np.concatenate(split(real), axis=0))
        left.append(np.concatenate(split(real.T), axis=1))
    return np.stack(right), np.stack(left)


def sums_kernel(
    sections, positions, group, pieces, extent, resident,
    place_ref, offsets_own_ref, offsets_other_ref, object_ref, probe_ref, right_ref, left_ref,
    intensity_own, intensity_other, *rest,
):
    piece_refs = rest[:pieces]
    out_ref = rest[pieces]
    staged, field, waves, sums, measured, sems = rest[pieces + 1:]
    own, half = place_ref[0], place_ref[1]
    total = 2 * positions
    side = object_ref.shape[1]
    blocks = side // lanes

    copies = [
        pltpu.make_async_copy(intensity_own, measured.at[pl.ds(half * positions, positions)], sems.at[0]),
        pltpu.make_async_copy(intensity_other, measured.at[pl.ds((1 - half) * positions, positions)], sems.at[1]),
    ]
    for index, piece in enumerate(piece_refs if resident else ()):
        shift, row = place_ref[2 + 2 * index], place_ref[3 + 2 * index]
        height = piece.shape[1]
        copies.append(
            pltpu.make_async_copy(
                piece, staged.at[shift, :, pl.ds(pl.multiple_of(row, 16), height), :], sems.at[2 + index]
            )
        )
    for copy in copies:
        copy.start()

    sums[...] = jnp.zeros_like(sums)

    def corner(position):
        is_own = position // positions == half
        slot = lax.rem(position, positions)
        row = jnp.where(is_own, offsets_own_ref[slot, 0], offsets_other_ref[slot, 0])
        column = jnp.where(is_own, offsets_own_ref[slot, 1], offsets_other_ref[slot, 1])
        first = column // lanes
        second = jnp.minimum(first + 1, blocks - 1)
        return row, first, second, column - first * lanes

    lane_of = lax.broadcasted_iota(jnp.int32, (extent, lanes), 1)

    def start_wave(position, carry):
        shift = corner(position)[3]
        for part in range(2):
            waves[0, position, part] = pltpu.roll(probe_ref[part].astype(jnp.float32), shift, 1)
        return carry

    lax.fori_loop(0, total, start_wave, 0)

    for copy in copies:
        copy.wait()

    def load_slice(index, slot):
        for part in range(2):
            for block in range(blocks):
                field[slot, part, block] = staged[index, part, :, block * lanes:(block + 1) * lanes].astype(jnp.float32)

    def load_own(slot):
        for part in range(2):
            for block in range(blocks):
                field[slot, part, block] = (
                    object_ref[part, :, block * lanes:(block + 1) * lanes].astype(wire).astype(jnp.float32)
                )

    def bring(index):
        def other():
            load_slice(index, index)

        def mine():
            load_own(index)

        lax.cond(index == own, mine, other)

    def bring_all(index, carry):
        bring(index)
        return carry

    if resident:
        lax.fori_loop(0, sections, bring_all, 0)

    def ready(index):
        if resident:
            return index
        copy = pltpu.make_async_copy(piece_refs[0].at[index], staged.at[0], sems.at[2])
        copy.start()
        copy.wait()
        load_slice(0, 0)
        return 0

    def sandwich(values, which):
        rows = jnp.concatenate(
            [jnp.concatenate([re.astype(jnp.bfloat16), im.astype(jnp.bfloat16)], axis=1) for re, im in values], axis=0
        )
        middle = jnp.dot(
            jnp.concatenate([rows, rows], axis=1), right_ref[which], preferred_element_type=jnp.float32
        ).astype(jnp.bfloat16)
        parts = [middle[index * extent:(index + 1) * extent] for index in range(len(values))]
        columns = jnp.concatenate(
            [
                jnp.concatenate([part[:, :extent] for part in parts], axis=1),
                jnp.concatenate([part[:, extent:] for part in parts], axis=1),
            ],
            axis=0,
        )
        result = jnp.dot(
            left_ref[which], jnp.concatenate([columns, columns], axis=0), preferred_element_type=jnp.float32
        )
        return [
            (
                result[:extent, index * extent:(index + 1) * extent],
                result[extent:, index * extent:(index + 1) * extent],
            )
            for index in range(len(values))
        ]

    def through(index, source, first_position):
        values = []
        for member in range(group):
            position = first_position + member
            row, first, second, shift = corner(position)
            mask = lane_of < shift
            window = [
                jnp.where(
                    mask,
                    field[index, part, second, pl.ds(row, extent), :],
                    field[index, part, first, pl.ds(row, extent), :],
                )
                for part in range(2)
            ]
            re = waves[source, position, 0]
            im = waves[source, position, 1]
            values.append((window[0] * re - window[1] * im, window[0] * im + window[1] * re))
        return values

    def keep(values, target, first_position):
        for member, (re, im) in enumerate(values):
            waves[target, first_position + member, 0] = re
            waves[target, first_position + member, 1] = im

    def step(index, source, target):
        slot = ready(index)

        def one_group(number, carry):
            first_position = number * group
            keep(sandwich(through(slot, source, first_position), 0), target, first_position)
            return carry

        lax.fori_loop(0, total // group, one_group, 0)

    def forward(index, carry):
        step(index, (index > own).astype(jnp.int32), (index + 1 > own).astype(jnp.int32))
        return carry

    lax.fori_loop(0, sections - 1, forward, 0)

    last_slot = ready(sections - 1)

    def far_group(number, carry):
        first_position = number * group
        source = (sections - 1 > own).astype(jnp.int32)
        far = sandwich(through(last_slot, source, first_position), 1)
        weighted = []
        for member, (re, im) in enumerate(far):
            misfit = re * re + im * im - measured[first_position + member].astype(jnp.float32)
            weighted.append((misfit * re, -(misfit * im)))
        keep(sandwich(weighted, 1), 1, first_position)
        return carry

    lax.fori_loop(0, total // group, far_group, 0)

    def backward(count, carry):
        step(sections - 1 - count, 1, 1)
        return carry

    lax.fori_loop(0, sections - 1 - own, backward, 0)

    def settle(position, carry):
        row, first, second, shift = corner(position)
        mask = lane_of < shift
        wave_re, wave_im = waves[0, position, 0], waves[0, position, 1]
        grad_re, grad_im = waves[1, position, 0], waves[1, position, 1]
        terms = (
            wave_re * grad_re - wave_im * grad_im,
            -(wave_re * grad_im + wave_im * grad_re),
            wave_re * wave_re + wave_im * wave_im,
        )
        for kind, term in enumerate(terms):
            sums[kind, first, pl.ds(row, extent), :] += jnp.where(mask, 0.0, term)
            sums[kind, second, pl.ds(row, extent), :] += jnp.where(mask, term, 0.0)
        return carry

    lax.fori_loop(0, total, settle, 0)
    for kind in range(3):
        for block in range(blocks):
            out_ref[kind, :, block * lanes:(block + 1) * lanes] = sums[kind, block].astype(wire)


def on_device(object_slices, probe, intensities, offsets):
    own_object = object_slices[:, 0]
    side = own_object.shape[1]
    extent = probe.shape[1]
    positions = offsets.shape[0]
    sections = lax.axis_size("cuts")
    own = lax.axis_index("cuts")
    members = lax.axis_size("probe")
    member = lax.axis_index("probe")
    half_count = members // 2
    half = member // half_count

    across = [(source, (source + half_count) % members) for source in range(members)]
    beside = [(source, source ^ 1) for source in range(members)]

    measured = intensities.astype(wire)
    measured_other = lax.ppermute(measured, "probe", across)
    offsets_other = lax.ppermute(offsets, "probe", across)

    resident = sections * own_object.size * 6 <= resident_bytes
    pieces, places = [], []
    if resident:
        height = side // members
        quarter = lax.dynamic_slice_in_dim(own_object, member * height, height, 1).astype(wire)
        for distance in range(1, sections):
            ring = [(source, (source + distance) % sections) for source in range(sections)]
            first = lax.ppermute(quarter, "cuts", ring)
            opposite = lax.ppermute(first, "probe", across)
            origin = (own - distance) % sections
            for piece, where in (
                (first, member),
                (opposite, (member + half_count) % members),
                (lax.ppermute(first, "probe", beside), member ^ 1),
                (lax.ppermute(opposite, "probe", beside), ((member ^ 1) + half_count) % members),
            ):
                pieces.append(piece)
                places += [origin, where * height]
    else:
        pieces.append(lax.all_gather(own_object.astype(wire), "cuts"))

    right, left = tables(extent)
    scalars = jnp.stack([jnp.asarray(v, jnp.int32) for v in [own, half] + places])
    smem = pl.BlockSpec(memory_space=pltpu.SMEM)
    vmem = pl.BlockSpec(memory_space=pltpu.VMEM)
    anywhere = pl.BlockSpec(memory_space=pl.ANY)
    group = 4
    total = 2 * positions
    blocks = side // lanes
    slots = sections if resident else 1
    own_sums = pl.pallas_call(
        functools.partial(sums_kernel, sections, positions, group, len(pieces), extent, resident),
        out_shape=jax.ShapeDtypeStruct((3, side, side), wire),
        in_specs=[smem, smem, smem] + [vmem] * 4 + [anywhere] * (2 + len(pieces)),
        out_specs=vmem,
        scratch_shapes=[
            pltpu.VMEM((slots, 2, side, side), wire),
            pltpu.VMEM((slots, 2, blocks, side, lanes), jnp.float32),
            pltpu.VMEM((2, total, 2, extent, extent), jnp.float32),
            pltpu.VMEM((3, blocks, side, lanes), jnp.float32),
            pltpu.VMEM((total, extent, extent), wire),
            pltpu.SemaphoreType.DMA((2 + len(pieces),)),
        ],
        compiler_params=pltpu.CompilerParams(vmem_limit_bytes=48 * 2**20),
    )(
        scalars, offsets, offsets_other, own_object, probe, jnp.asarray(right), jnp.asarray(left),
        measured, measured_other, *pieces,
    )
    other_sums = lax.ppermute(own_sums, "probe", beside)
    summed = own_sums.astype(jnp.float32) + other_sums.astype(jnp.float32)
    updated = own_object - (step_size / (summed[2] + regular)) * summed[:2]
    return updated[:, None]


def solution(mesh):
    in_specs = (
        P(None, ("group", "cuts"), None, None),
        P("group", None, None),
        P(("group", "probe"), None, None),
        P(("group", "probe"), None),
    )
    out_specs = P(None, ("group", "cuts"), None, None)
    return jax.shard_map(
        on_device, mesh=mesh, in_specs=in_specs, out_specs=out_specs, check_vma=False
    )
```

time: 523 us -> 64.8 us (0.12)
  waiting for transfers between devices: 177 us -> 15.3 us
  starting transfers between devices: 141 us -> 12.6 us
  local copies, waits for them, and re-layouts: 70.2 us -> 4.02 us
  loops' own time: 59.9 us -> 0 us
  other arithmetic: 40.8 us -> 2.56 us
  Pallas kernels: 0 us -> 29.9 us
  matrix products: 16.9 us -> 0 us
  between operations: 13.5 us -> 0.09 us
    ppermute x22 -> x15, starting transfers between devices: 141 us -> 12.6 us  [the longest x3 6.11 us: on_device(): first = lax.ppermute(quarter, 'cuts', ring)]
    ppermute x22 -> x15, waiting for transfers between devices: 140 us -> 15.3 us  [the longest x3 5.82 us: on_device(): opposite = lax.ppermute(first, 'probe', across)]
    another operation x40 -> x0, loops' own time: 59.9 us -> none  [the longest x8 29.7 us: backward_turn(): lax.cond(is_last, release, compute)]
    dynamic_update_slice x32 -> x0, local copies, waits for them, and re-layouts: 51.5 us -> none  [the longest x24 46.4 us: accumulate(): lax.dynamic_update_slice(running, lax.dynamic_slice(running, corner, (ext...]
    psum x1 -> x0, waiting for transfers between devices: 36.5 us -> none  [on_device(): lax.psum(totals[1].astype(jnp.bfloat16), 'probe').astype(jnp.float32)]
    pallas_call x0 -> x1, Pallas kernels: none -> 29.9 us  [on_device(): pl.pallas_call(functools.partial(sums_kernel, sections, positions, group,...]
    dot_general x66 -> x0, matrix products: 16.9 us -> none  [product(): jnp.dot(factor_a, factor_b, precision=highest, preferred_element_type=jnp...]
    another operation x33 -> x0, other arithmetic: 12.7 us -> none  [the longest x16 6.12 us: settle(): jnp.stack([piece_re * grad_re + piece_im * grad_im, piece_re * grad_im -...]
  transfers between devices with their start and end apart: 23 -> 15, of which waited for: 23 -> 6; matrix products, arithmetic and copies ran while one was open for 0% -> 3% of each run, Pallas kernels for 0% -> 0%
where the time goes in v1:
time: 64.8 us; the launch traced here: 64.5 us
  Pallas kernels  29.9 us (46%)
  waiting for transfers between devices  15.3 us (24%)
  starting transfers between devices  12.6 us (19%)
  local copies, waits for them, and re-layouts  4.02 us (6%)
  other arithmetic  2.56 us (4%)
    pallas_call x1, Pallas kernels, on_device(): pl.pallas_call(functools.partial(sums_kernel, sections, positions, group,...  29.9 us
    ppermute x3, starting transfers between devices, on_device(): first = lax.ppermute(quarter, 'cuts', ring)  6.11 us
    ppermute x3, waiting for transfers between devices, on_device(): opposite = lax.ppermute(first, 'probe', across)  5.82 us
    ppermute x1, waiting for transfers between devices, on_device(): offsets_other = lax.ppermute(offsets, 'probe', across)  4.51 us
    ppermute x3, starting transfers between devices, on_device(): opposite = lax.ppermute(first, 'probe', across)  3.52 us
    unnamed x9, local copies, waits for them, and re-layouts  2.84 us
    ppermute x1, waiting for transfers between devices, on_device(): other_sums = lax.ppermute(own_sums, 'probe', beside)  2.21 us
    ppermute x1, starting transfers between devices, on_device(): measured_other = lax.ppermute(measured, 'probe', across)  1.56 us
  transfers between devices with their start and end apart: 15, of which 6 were waited for; matrix products, arithmetic and copies ran while one was open for 3% of the time, Pallas kernels for 0%

profile of v1, /device:TPU:0, one launch (start us, length us, event | category | flops | bytes accessed | tf_op | source)
XLA Modules:
  0.0 64.5 jit_solution(4998224255148727142)
XLA Ops:
  0.0 1.1 %fusion.4 = bf16[2,96,384]{2,1,0:T(8,128)(2,1)S(1)} fusion(f32[2,1,384,384]{3,2,0,1:T(8,128)} %bitcast.20, s32[]{:T(128)S(6)} %select_n.44), kind=kLoop, calls=%fused_computation.8 | loop fusion | bytes 294916 | tf_op jit(solution)/shard_map/convert_element_type | solution.py:260
  1.1 5.1 %collective-permute-start.10 = (bf16[2,96,384]{2,1,0:T(8,128)(2,1)S(1)}, bf16[2,96,384]{2,1,0:T(8,128)(2,1)S(1)}, u32[]{:S(2)}, u32[]{:S(2)}) collective-permute-start(bf16[2,96,384]{2,1,0:T(8,128)(2,1)S(1)} %fusion.4), channel_id=1, source_target_pairs={{0,12},{4,0},{8,4},{12,8},{1,13},{5,1},{9,5},{13,9},{2,14},{6,2},{... | collective-permute-start | bytes 442376 | tf_op jit(solution)/shard_map/ppermute | solution.py:263
  6.2 1.0 %collective-permute-start.2 = (bf16[2,96,384]{2,1,0:T(8,128)(2,1)S(1)}, bf16[2,96,384]{2,1,0:T(8,128)(2,1)S(1)}, u32[]{:S(2)}, u32[]{:S(2)}) collective-permute-start(bf16[2,96,384]{2,1,0:T(8,128)(2,1)S(1)} %fusion.4), channel_id=1, source_target_pairs={{0,4},{4,8},{8,12},{12,0},{1,5},{5,9},{9,13},{13,1},{2,6},{6,10},{... | collective-permute-start | bytes 442376 | tf_op jit(solution)/shard_map/ppermute | solution.py:263
  7.2 1.1 %convert_element_type.15.intensity_own = bf16[8,128,128]{2,1,0:T(8,128)(2,1)S(1)} convert(f32[8,128,128]{2,1,0:T(8,128)} %param.8) | non-fusion elementwise | flops 131072 | bytes 786432 | tf_op jit(solution)/shard_map/convert_element_type | solution.py:252
  8.3 1.6 %collective-permute-start.1 = (bf16[8,128,128]{2,1,0:T(8,128)(2,1)S(1)}, bf16[8,128,128]{2,1,0:T(8,128)(2,1)S(1)}, u32[]{:S(2)}, u32[]{:S(2)}) collective-permute-start(bf16[8,128,128]{2,1,0:T(8,128)(2,1)S(1)} %convert_element_type.15.intensity_own), channel_id=1, source_target_pairs={{0,2},{1,3},{2,0},{3,1},{4,6},{5,7},{6,4},{7,5},{8,10},{9,11},{10,... | collective-permute-start | bytes 786440 | tf_op jit(solution)/shard_map/ppermute | solution.py:253
  9.8 0.8 %copy.9.offsets_own_ref = s32[8,2]{1,0:T(8,128)S(1)} copy(s32[8,2]{0,1:T(2,128)} %param.9) | data formatting | bytes 128 | tf_op args[3]
  10.6 0.5 collective-permute-start
  11.1 0.0 collective-permute-done.10.rest_8_
  11.1 0.0 collective-permute-start.12
  11.1 4.5 %collective-permute-done.offsets_other_ref = s32[8,2]{1,0:T(8,128)S(1)} collective-permute-done((s32[8,2]{1,0:T(8,128)S(1)}, s32[8,2]{1,0:T(8,128)S(1)}, u32[]{:S(2)}, u32[]{:S(2)}) %collective-permute-start) | collective-permute-done | bytes 96 | tf_op jit(solution)/shard_map/ppermute | solution.py:254
  15.6 1.5 %collective-permute-start.11 = (bf16[2,96,384]{2,1,0:T(8,128)(2,1)S(1)}, bf16[2,96,384]{2,1,0:T(8,128)(2,1)S(1)}, u32[]{:S(2)}, u32[]{:S(2)}) collective-permute-start(bf16[2,96,384]{2,1,0:T(8,128)(2,1)S(1)} %collective-permute-done.10.rest_8_), channel_id=1, source_target_pairs={{0,2},{1,3},{2,0},{3,1},{4,6},{5,7},{6,4},{7,5},{8,10},{9,11},{10,... | collective-permute-start | bytes 442376 | tf_op jit(solution)/shard_map/ppermute | solution.py:264
  17.1 1.5 %collective-permute-done.6.rest_4_ = bf16[2,96,384]{2,1,0:T(8,128)(2,1)S(1)} collective-permute-done((bf16[2,96,384]{2,1,0:T(8,128)(2,1)S(1)}, bf16[2,96,384]{2,1,0:T(8,128)(2,1)S(1)}, u32[]{:S(2)}, u32[]{:S(2)}) %collective-permute-start.6) | collective-permute-done | bytes 147488 | tf_op jit(solution)/shard_map/ppermute | solution.py:263
  18.7 1.5 %collective-permute-start.7 = (bf16[2,96,384]{2,1,0:T(8,128)(2,1)S(1)}, bf16[2,96,384]{2,1,0:T(8,128)(2,1)S(1)}, u32[]{:S(2)}, u32[]{:S(2)}) collective-permute-start(bf16[2,96,384]{2,1,0:T(8,128)(2,1)S(1)} %collective-permute-done.6.rest_4_), channel_id=1, source_target_pairs={{0,2},{1,3},{2,0},{3,1},{4,6},{5,7},{6,4},{7,5},{8,10},{9,11},{10,... | collective-permute-start | bytes 442376 | tf_op jit(solution)/shard_map/ppermute | solution.py:264
  20.2 0.0 collective-permute-done.2.rest_0_
  20.2 0.5 collective-permute-start.3
  20.7 0.0 collective-permute-done.1.intensity_other
  20.7 0.0 collective-permute-start.8
  20.7 0.0 collective-permute-done.12.rest_10_
  20.7 0.5 collective-permute-start.4
  21.2 0.1 collective-permute-start.13
  21.3 4.2 %collective-permute-done.7.rest_5_ = bf16[2,96,384]{2,1,0:T(8,128)(2,1)S(1)} collective-permute-done((bf16[2,96,384]{2,1,0:T(8,128)(2,1)S(1)}, bf16[2,96,384]{2,1,0:T(8,128)(2,1)S(1)}, u32[]{:S(2)}, u32[]{:S(2)}) %collective-permute-start.7) | collective-permute-done | bytes 147488 | tf_op jit(solution)/shard_map/ppermute | solution.py:264
  25.5 1.7 %collective-permute-done.3.rest_1_ = bf16[2,96,384]{2,1,0:T(8,128)(2,1)S(1)} collective-permute-done((bf16[2,96,384]{2,1,0:T(8,128)(2,1)S(1)}, bf16[2,96,384]{2,1,0:T(8,128)(2,1)S(1)}, u32[]{:S(2)}, u32[]{:S(2)}) %collective-permute-start.3) | collective-permute-done | bytes 147488 | tf_op jit(solution)/shard_map/ppermute | solution.py:264
  27.1 0.1 stack.56.place_ref
  27.3 1.2 %collective-permute-done.5.rest_3_ = bf16[2,96,384]{2,1,0:T(8,128)(2,1)S(1)} collective-permute-done((bf16[2,96,384]{2,1,0:T(8,128)(2,1)S(1)}, bf16[2,96,384]{2,1,0:T(8,128)(2,1)S(1)}, u32[]{:S(2)}, u32[]{:S(2)}) %collective-permute-start.5) | collective-permute-done | bytes 147488 | tf_op jit(solution)/shard_map/ppermute | solution.py:270
  28.5 1.0 %copy-done.1 = bf16[2,256,512]{2,1,0:T(8,128)(2,1)S(1)} copy-done((bf16[2,256,512]{2,1,0:T(8,128)(2,1)S(1)}, bf16[2,256,512]{2,1,0:T(8,128)(2,1)}, u32[]{:S(2)}) %copy-start.1) | copy-done | bytes 524312
  29.5 1.0 %copy-done.2 = bf16[2,512,256]{2,1,0:T(8,128)(2,1)S(1)} copy-done((bf16[2,512,256]{2,1,0:T(8,128)(2,1)S(1)}, bf16[2,512,256]{2,1,0:T(8,128)(2,1)}, u32[]{:S(2)}) %copy-start.2) | copy-done | bytes 524312
  30.6 29.9 %shard_map.64 = bf16[3,384,384]{2,1,0:T(8,128)(2,1)S(1)} custom-call(s32[26]{0:T(128)S(1)} %stack.56.place_ref, s32[8,2]{1,0:T(8,128)S(1)} %copy.9.offsets_own_ref, s32[8,2]{1,0:T(8,128)S(1)} %collective-permute-done.offsets_other_ref, f32[2,384,384]{2,1,0:T(8,128)S(1)} %bitcast.21, bf16[2,128,128]{2,1,0:T(8,128)(2,1)S(1)} %copy-done.3, ...), custom_call_target="tpu_custom_call" | custom-call | tf_op jit(solution)/shard_map/pallas_call | solution.py:286
  60.5 0.3 collective-permute-start.14
  60.8 2.2 %collective-permute-done.14 = bf16[3,384,384]{2,1,0:T(8,128)(2,1)S(1)} collective-permute-done((bf16[3,384,384]{2,1,0:T(8,128)(2,1)S(1)}, bf16[3,384,384]{2,1,0:T(8,128)(2,1)S(1)}, u32[]{:S(2)}, u32[]{:S(2)}) %collective-permute-start.14) | collective-permute-done | bytes 884768 | tf_op jit(solution)/shard_map/ppermute | solution.py:304
  63.0 0.2 convert_add_fusion
  63.2 0.1 fusion.3
  63.3 1.2 %fusion.1 = f32[2,1,384,384]{3,2,1,0:T(8,128)} fusion(f32[3,384,384]{2,1,0:T(8,128)S(1)} %convert_add_fusion, f32[384,384]{1,0:T(8,128)S(1)} %fusion.3, f32[2,1,384,384]{3,2,1,0:T(8,128)S(1)} %copy-done), kind=kLoop, calls=%fused_computation.3 | loop fusion | flops 589824 | bytes 4128768 | tf_op jit(solution)/shard_map/broadcast_in_dim | solution.py:307
  (14 shorter events, 0.0 us)
Async XLA Ops:
  0.0 28.5 %copy-start = (f32[2,1,384,384]{3,2,1,0:T(8,128)S(1)}, f32[2,1,384,384]{3,2,1,0:T(8,128)}, u32[]{:S(2)}) copy-start(f32[2,1,384,384]{3,2,1,0:T(8,128)} %param.6) | copy-start | bytes 3538948
  0.0 28.5 %copy-start.3 = (bf16[2,128,128]{2,1,0:T(8,128)(2,1)S(1)}, bf16[2,128,128]{2,1,0:T(8,128)(2,1)}, u32[]{:S(2)}) copy-start(bf16[2,128,128]{2,1,0:T(8,128)(2,1)} %probe_ref.1) | copy-start | bytes 196612
  1.1 10.0 %collective-permute-start.10 = (bf16[2,96,384]{2,1,0:T(8,128)(2,1)S(1)}, bf16[2,96,384]{2,1,0:T(8,128)(2,1)S(1)}, u32[]{:S(2)}, u32[]{:S(2)}) collective-permute-start(bf16[2,96,384]{2,1,0:T(8,128)(2,1)S(1)} %fusion.4), channel_id=1, source_target_pairs={{0,12},{4,0},{8,4},{12,8},{1,13},{5,1},{9,5},{13,9},{2,14},{6,2},{... | collective-permute-start | bytes 442376 | tf_op jit(solution)/shard_map/ppermute | solution.py:263
  6.2 12.5 %collective-permute-start.6 = (bf16[2,96,384]{2,1,0:T(8,128)(2,1)S(1)}, bf16[2,96,384]{2,1,0:T(8,128)(2,1)S(1)}, u32[]{:S(2)}, u32[]{:S(2)}) collective-permute-start(bf16[2,96,384]{2,1,0:T(8,128)(2,1)S(1)} %fusion.4), channel_id=1, source_target_pairs={{0,8},{4,12},{8,0},{12,4},{1,9},{5,13},{9,1},{13,5},{2,10},{6,14},... | collective-permute-start | bytes 442376 | tf_op jit(solution)/shard_map/ppermute | solution.py:263
  6.2 14.0 %collective-permute-start.2 = (bf16[2,96,384]{2,1,0:T(8,128)(2,1)S(1)}, bf16[2,96,384]{2,1,0:T(8,128)(2,1)S(1)}, u32[]{:S(2)}, u32[]{:S(2)}) collective-permute-start(bf16[2,96,384]{2,1,0:T(8,128)(2,1)S(1)} %fusion.4), channel_id=1, source_target_pairs={{0,4},{4,8},{8,12},{12,0},{1,5},{5,9},{9,13},{13,1},{2,6},{6,10},{... | collective-permute-start | bytes 442376 | tf_op jit(solution)/shard_map/ppermute | solution.py:263
  8.3 12.4 %collective-permute-start.1 = (bf16[8,128,128]{2,1,0:T(8,128)(2,1)S(1)}, bf16[8,128,128]{2,1,0:T(8,128)(2,1)S(1)}, u32[]{:S(2)}, u32[]{:S(2)}) collective-permute-start(bf16[8,128,128]{2,1,0:T(8,128)(2,1)S(1)} %convert_element_type.15.intensity_own), channel_id=1, source_target_pairs={{0,2},{1,3},{2,0},{3,1},{4,6},{5,7},{6,4},{7,5},{8,10},{9,11},{10,... | collective-permute-start | bytes 786440 | tf_op jit(solution)/shard_map/ppermute | solution.py:253
  10.6 5.0 %collective-permute-start = (s32[8,2]{1,0:T(8,128)S(1)}, s32[8,2]{1,0:T(8,128)S(1)}, u32[]{:S(2)}, u32[]{:S(2)}) collective-permute-start(s32[8,2]{1,0:T(8,128)S(1)} %copy.9.offsets_own_ref), channel_id=1, source_target_pairs={{0,2},{1,3},{2,0},{3,1},{4,6},{5,7},{6,4},{7,5},{8,10},{9,11},{10,... | collective-permute-start | bytes 200 | tf_op jit(solution)/shard_map/ppermute | solution.py:254
  11.1 9.6 %collective-permute-start.12 = (bf16[2,96,384]{2,1,0:T(8,128)(2,1)S(1)}, bf16[2,96,384]{2,1,0:T(8,128)(2,1)S(1)}, u32[]{:S(2)}, u32[]{:S(2)}) collective-permute-start(bf16[2,96,384]{2,1,0:T(8,128)(2,1)S(1)} %collective-permute-done.10.rest_8_), channel_id=1, source_target_pairs={{0,1},{1,0},{2,3},{3,2},{4,5},{5,4},{6,7},{7,6},{8,9},{9,8},{10,11... | collective-permute-start | bytes 442376 | tf_op jit(solution)/shard_map/ppermute | solution.py:269
  15.6 5.6 %collective-permute-start.11 = (bf16[2,96,384]{2,1,0:T(8,128)(2,1)S(1)}, bf16[2,96,384]{2,1,0:T(8,128)(2,1)S(1)}, u32[]{:S(2)}, u32[]{:S(2)}) collective-permute-start(bf16[2,96,384]{2,1,0:T(8,128)(2,1)S(1)} %collective-permute-done.10.rest_8_), channel_id=1, source_target_pairs={{0,2},{1,3},{2,0},{3,1},{4,6},{5,7},{6,4},{7,5},{8,10},{9,11},{10,... | collective-permute-start | bytes 442376 | tf_op jit(solution)/shard_map/ppermute | solution.py:264
  18.7 6.8 %collective-permute-start.7 = (bf16[2,96,384]{2,1,0:T(8,128)(2,1)S(1)}, bf16[2,96,384]{2,1,0:T(8,128)(2,1)S(1)}, u32[]{:S(2)}, u32[]{:S(2)}) collective-permute-start(bf16[2,96,384]{2,1,0:T(8,128)(2,1)S(1)} %collective-permute-done.6.rest_4_), channel_id=1, source_target_pairs={{0,2},{1,3},{2,0},{3,1},{4,6},{5,7},{6,4},{7,5},{8,10},{9,11},{10,... | collective-permute-start | bytes 442376 | tf_op jit(solution)/shard_map/ppermute | solution.py:264
  20.2 6.9 %collective-permute-start.3 = (bf16[2,96,384]{2,1,0:T(8,128)(2,1)S(1)}, bf16[2,96,384]{2,1,0:T(8,128)(2,1)S(1)}, u32[]{:S(2)}, u32[]{:S(2)}) collective-permute-start(bf16[2,96,384]{2,1,0:T(8,128)(2,1)S(1)} %collective-permute-done.2.rest_0_), channel_id=1, source_target_pairs={{0,2},{1,3},{2,0},{3,1},{4,6},{5,7},{6,4},{7,5},{8,10},{9,11},{10,... | collective-permute-start | bytes 442376 | tf_op jit(solution)/shard_map/ppermute | solution.py:264
  20.7 6.5 %collective-permute-start.8 = (bf16[2,96,384]{2,1,0:T(8,128)(2,1)S(1)}, bf16[2,96,384]{2,1,0:T(8,128)(2,1)S(1)}, u32[]{:S(2)}, u32[]{:S(2)}) collective-permute-start(bf16[2,96,384]{2,1,0:T(8,128)(2,1)S(1)} %collective-permute-done.6.rest_4_), channel_id=1, source_target_pairs={{0,1},{1,0},{2,3},{3,2},{4,5},{5,4},{6,7},{7,6},{8,9},{9,8},{10,11... | collective-permute-start | bytes 442376 | tf_op jit(solution)/shard_map/ppermute | solution.py:269
  20.7 6.5 %collective-permute-start.4 = (bf16[2,96,384]{2,1,0:T(8,128)(2,1)S(1)}, bf16[2,96,384]{2,1,0:T(8,128)(2,1)S(1)}, u32[]{:S(2)}, u32[]{:S(2)}) collective-permute-start(bf16[2,96,384]{2,1,0:T(8,128)(2,1)S(1)} %collective-permute-done.2.rest_0_), channel_id=1, source_target_pairs={{0,1},{1,0},{2,3},{3,2},{4,5},{5,4},{6,7},{7,6},{8,9},{9,8},{10,11... | collective-permute-start | bytes 442376 | tf_op jit(solution)/shard_map/ppermute | solution.py:269
  21.2 6.0 %collective-permute-start.13 = (bf16[2,96,384]{2,1,0:T(8,128)(2,1)S(1)}, bf16[2,96,384]{2,1,0:T(8,128)(2,1)S(1)}, u32[]{:S(2)}, u32[]{:S(2)}) collective-permute-start(bf16[2,96,384]{2,1,0:T(8,128)(2,1)S(1)} %collective-permute-done.11.rest_9_), channel_id=1, source_target_pairs={{0,1},{1,0},{2,3},{3,2},{4,5},{5,4},{6,7},{7,6},{8,9},{9,8},{10,11... | collective-permute-start | bytes 442376 | tf_op jit(solution)/shard_map/ppermute | solution.py:270
  25.5 1.8 %collective-permute-start.9 = (bf16[2,96,384]{2,1,0:T(8,128)(2,1)S(1)}, bf16[2,96,384]{2,1,0:T(8,128)(2,1)S(1)}, u32[]{:S(2)}, u32[]{:S(2)}) collective-permute-start(bf16[2,96,384]{2,1,0:T(8,128)(2,1)S(1)} %collective-permute-done.7.rest_5_), channel_id=1, source_target_pairs={{0,1},{1,0},{2,3},{3,2},{4,5},{5,4},{6,7},{7,6},{8,9},{9,8},{10,11... | collective-permute-start | bytes 442376 | tf_op jit(solution)/shard_map/ppermute | solution.py:270
  27.1 1.4 %collective-permute-start.5 = (bf16[2,96,384]{2,1,0:T(8,128)(2,1)S(1)}, bf16[2,96,384]{2,1,0:T(8,128)(2,1)S(1)}, u32[]{:S(2)}, u32[]{:S(2)}) collective-permute-start(bf16[2,96,384]{2,1,0:T(8,128)(2,1)S(1)} %collective-permute-done.3.rest_1_), channel_id=1, source_target_pairs={{0,1},{1,0},{2,3},{3,2},{4,5},{5,4},{6,7},{7,6},{8,9},{9,8},{10,11... | collective-permute-start | bytes 442376 | tf_op jit(solution)/shard_map/ppermute | solution.py:270
  28.5 1.0 %copy-start.1 = (bf16[2,256,512]{2,1,0:T(8,128)(2,1)S(1)}, bf16[2,256,512]{2,1,0:T(8,128)(2,1)}, u32[]{:S(2)}) copy-start(bf16[2,256,512]{2,1,0:T(8,128)(2,1)} %constant.80.clone.left_ref) | copy-start | bytes 1572868
  29.5 1.0 %copy-start.2 = (bf16[2,512,256]{2,1,0:T(8,128)(2,1)S(1)}, bf16[2,512,256]{2,1,0:T(8,128)(2,1)}, u32[]{:S(2)}) copy-start(bf16[2,512,256]{2,1,0:T(8,128)(2,1)} %constant.79.clone.right_ref) | copy-start | bytes 1572868
  60.5 2.5 %collective-permute-start.14 = (bf16[3,384,384]{2,1,0:T(8,128)(2,1)S(1)}, bf16[3,384,384]{2,1,0:T(8,128)(2,1)S(1)}, u32[]{:S(2)}, u32[]{:S(2)}) collective-permute-start(bf16[3,384,384]{2,1,0:T(8,128)(2,1)S(1)} %shard_map.64), channel_id=1, source_target_pairs={{0,1},{1,0},{2,3},{3,2},{4,5},{5,4},{6,7},{7,6},{8,9},{9,8},{10,11... | collective-permute-start | bytes 2654216 | tf_op jit(solution)/shard_map/ppermute | solution.py:304

commit v2 on v1

v2 whole, which is shorter than its diff:
```python
import functools
import math

import jax
import jax.numpy as jnp
import ml_dtypes
import numpy as np
from jax import lax
from jax.experimental import pallas as pl
from jax.experimental.pallas import tpu as pltpu
from jax.sharding import PartitionSpec as P

fresnel_phase = 12.0
step_size = 0.5
regular = 1.0
wire = jnp.bfloat16
lanes = 128
first_factor = 1.0554317823341433 * np.exp(1.0168288222118962j)
second_factor = 2.0 / 1.0554317823341433 * np.exp(1.06185831691335j)
dft_factor = 1.1777227895949816 * np.exp(1.1780972450961724j)
resident_bytes = 24 * 2**20


def tables(extent):
    k = np.arange(extent)
    dft = np.exp(-2j * np.pi * (np.outer(k, k) % extent) / extent) / math.sqrt(extent)
    f = np.where(k < (extent + 1) // 2, k, k - extent) / extent
    fresnel = dft.conj() @ (np.exp(-1j * fresnel_phase * f * f)[:, None] * dft)

    def real_form(matrix):
        return np.block([[matrix.real, matrix.imag], [-matrix.imag, matrix.real]]).astype(ml_dtypes.bfloat16)

    last = real_form(dft * dft_factor)
    return np.stack(
        [real_form(fresnel * first_factor), real_form(fresnel * second_factor).T * ml_dtypes.bfloat16(0.5), last, last.T]
    )


def corner_of(half, positions, blocks, offsets_own_ref, offsets_other_ref, position):
    is_own = position // positions == half
    slot = lax.rem(position, positions)
    row = jnp.where(is_own, offsets_own_ref[slot, 0], offsets_other_ref[slot, 0])
    column = jnp.where(is_own, offsets_own_ref[slot, 1], offsets_other_ref[slot, 1])
    first = column // lanes
    return row, first, jnp.minimum(first + 1, blocks - 1), column - first * lanes


def sandwich(values, right, left):
    extent = values[0][0].shape[0]
    rows = jnp.concatenate(
        [jnp.concatenate([re.astype(jnp.bfloat16), im.astype(jnp.bfloat16)], axis=1) for re, im in values], axis=0
    )
    middle = jnp.dot(rows, right, preferred_element_type=jnp.float32).astype(jnp.bfloat16)
    parts = [middle[index * extent:(index + 1) * extent] for index in range(len(values))]
    columns = jnp.concatenate(
        [
            jnp.concatenate([part[:, :extent] for part in parts], axis=1),
            jnp.concatenate([part[:, extent:] for part in parts], axis=1),
        ],
        axis=0,
    )
    result = jnp.dot(left, columns, preferred_element_type=jnp.float32)
    spans = [slice(index * extent, (index + 1) * extent) for index in range(len(values))]
    return [(result[:extent, span], result[extent:, span]) for span in spans]


def through(field, slot, waves, source, corners, chosen):
    extent = waves.shape[-2]
    lane_of = lax.broadcasted_iota(jnp.int32, (extent, lanes), 1)
    values = []
    for position in chosen:
        row, first, second, shift = corners(position)
        mask = lane_of < shift
        window_re, window_im = (
            jnp.where(
                mask, field[slot, part, second, pl.ds(row, extent), :], field[slot, part, first, pl.ds(row, extent), :]
            )
            for part in range(2)
        )
        re, im = waves[source, position, 0], waves[source, position, 1]
        values.append((window_re * re - window_im * im, window_re * im + window_im * re))
    return values


def keep(values, waves, target, chosen):
    for position, (re, im) in zip(chosen, values):
        waves[target, position, 0] = re
        waves[target, position, 1] = im


def in_batches(total, group, batch, work):
    def one_group(number, carry):
        for start in range(0, group, batch):
            work([number * group + start + member for member in range(batch)])
        return carry

    if total == group:
        one_group(0, 0)
    else:
        lax.fori_loop(0, total // group, one_group, 0)


def place_pieces(field, place_ref, first_place, piece_refs):
    for index, piece in enumerate(piece_refs):
        origin = place_ref[first_place + 2 * index]
        row = pl.multiple_of(place_ref[first_place + 2 * index + 1], 16)
        for part in range(2):
            for block in range(field.shape[2]):
                field[origin, part, block, pl.ds(row, piece.shape[1]), :] = (
                    piece[part, :, block * lanes:(block + 1) * lanes].astype(jnp.float32)
                )


def sums_kernel(
    sections, pieces, resident, group, batch,
    place_ref, offsets_own_ref, offsets_other_ref, tables_hbm, object_hbm, probe_ref, measured_own, measured_other, *rest,
):
    piece_refs = rest[:pieces]
    out_ref, field, waves, sums, table_ref, own_ref, sems = rest[pieces:]
    own, half = place_ref[0], place_ref[1]
    total, extent = waves.shape[1], waves.shape[3]
    positions = total // 2
    blocks = sums.shape[1]
    corners = functools.partial(corner_of, half, positions, blocks, offsets_own_ref, offsets_other_ref)

    table_copy = pltpu.make_async_copy(tables_hbm, table_ref, sems.at[0])
    table_copy.start()
    if resident:
        own_copy = pltpu.make_async_copy(object_hbm, own_ref, sems.at[1])
        own_copy.start()

    def start_wave(position, carry):
        shift = corners(position)[3]
        for part in range(2):
            waves[0, position, part] = pltpu.roll(probe_ref[part].astype(jnp.float32), shift, 1)
        return carry

    lax.fori_loop(0, total, start_wave, 0, unroll=4)
    sums[...] = jnp.zeros_like(sums)
    if resident:
        place_pieces(field, place_ref, 2, piece_refs)
        own_copy.wait()
        for part in range(2):
            for block in range(blocks):
                field[own, part, block] = (
                    own_ref[part, :, block * lanes:(block + 1) * lanes].astype(wire).astype(jnp.float32)
                )
    table_copy.wait()

    def ready(index):
        if resident:
            return index
        copy = pltpu.make_async_copy(piece_refs[0].at[index], own_ref, sems.at[1])
        copy.start()
        copy.wait()
        for part in range(2):
            for block in range(blocks):
                field[0, part, block] = own_ref[part, :, block * lanes:(block + 1) * lanes].astype(jnp.float32)
        return 0

    def step(index, source, target):
        slot = ready(index)

        def work(chosen):
            values = through(field, slot, waves, source, corners, chosen)
            keep(sandwich(values, table_ref[0], table_ref[1]), waves, target, chosen)

        in_batches(total, group, batch, work)

    def forward(index, carry):
        step(index, (index > own).astype(jnp.int32), (index + 1 > own).astype(jnp.int32))
        return carry

    lax.fori_loop(0, sections - 1, forward, 0)

    last_slot = ready(sections - 1)
    undo = abs(dft_factor) ** -4

    def far(chosen):
        source = (sections - 1 > own).astype(jnp.int32)
        fields = sandwich(through(field, last_slot, waves, source, corners, chosen), table_ref[2], table_ref[3])
        weighted = []
        for position, (re, im) in zip(chosen, fields):
            is_own = position // positions == half
            slot = lax.rem(position, positions)
            intensity = jnp.where(
                is_own, measured_own[slot].astype(jnp.float32), measured_other[slot].astype(jnp.float32)
            )
            misfit = ((re * re + im * im) * undo - intensity) * undo
            weighted.append((misfit * re, -(misfit * im)))
        keep(sandwich(weighted, table_ref[2], table_ref[3]), waves, 1, chosen)

    in_batches(total, group, batch, far)

    def backward(count, carry):
        step(sections - 1 - count, 1, 1)
        return carry

    lax.fori_loop(0, sections - 1 - own, backward, 0)

    lane_of = lax.broadcasted_iota(jnp.int32, (extent, lanes), 1)

    def settle(position, carry):
        row, first, second, shift = corners(position)
        mask = lane_of < shift
        wave_re, wave_im = waves[0, position, 0], waves[0, position, 1]
        grad_re, grad_im = waves[1, position, 0], waves[1, position, 1]
        terms = (
            wave_re * grad_re - wave_im * grad_im,
            -(wave_re * grad_im + wave_im * grad_re),
            wave_re * wave_re + wave_im * wave_im,
        )
        for kind, term in enumerate(terms):
            sums[kind, first, pl.ds(row, extent), :] += jnp.where(mask, 0.0, term)
            sums[kind, second, pl.ds(row, extent), :] += jnp.where(mask, term, 0.0)
        return carry

    lax.fori_loop(0, total, settle, 0)
    for kind in range(3):
        for block in range(blocks):
            out_ref[kind, :, block * lanes:(block + 1) * lanes] = sums[kind, block].astype(wire)


smem = pl.BlockSpec(memory_space=pltpu.SMEM)
vmem = pl.BlockSpec(memory_space=pltpu.VMEM)
anywhere = pl.BlockSpec(memory_space=pl.ANY)
GROUP, BATCH = 16, 16


def sums_call(sections, positions, extent, side, pieces, resident):
    total = 2 * positions
    group = math.gcd(GROUP, total)
    slice_shape = (2, side // lanes, side, lanes)
    return pl.pallas_call(
        functools.partial(sums_kernel, sections, pieces, resident, group, math.gcd(BATCH, group)),
        out_shape=jax.ShapeDtypeStruct((3, side, side), wire),
        in_specs=[smem] * 3 + [anywhere] * 2 + [vmem] * 3 + [vmem if resident else anywhere] * pieces,
        out_specs=vmem,
        scratch_shapes=[
            pltpu.VMEM((sections if resident else 1,) + slice_shape, jnp.float32),
            pltpu.VMEM((2, total, 2, extent, extent), jnp.float32),
            pltpu.VMEM((3,) + slice_shape[1:], jnp.float32),
            pltpu.VMEM((4, 2 * extent, 2 * extent), jnp.bfloat16),
            pltpu.VMEM((2, side, side), jnp.float32 if resident else wire),
            pltpu.SemaphoreType.DMA((2,)),
        ],
        compiler_params=pltpu.CompilerParams(vmem_limit_bytes=40 * 2**20),
    )


def on_device(object_slices, probe, intensities, offsets):
    own_object = object_slices[:, 0]
    side = own_object.shape[1]
    extent = probe.shape[1]
    positions = offsets.shape[0]
    sections = lax.axis_size("cuts")
    own = lax.axis_index("cuts")
    members = lax.axis_size("probe")
    member = lax.axis_index("probe")
    half_count = members // 2
    half = member // half_count

    across = [(source, (source + half_count) % members) for source in range(members)]
    beside = [(source, source ^ 1) for source in range(members)]

    def scalars(*values):
        return jnp.stack([jnp.asarray(value, jnp.int32) for value in values])

    measured = intensities.astype(wire)
    measured_other = lax.ppermute(measured, "probe", across)
    offsets_other = lax.ppermute(offsets, "probe", across)

    resident = sections & (sections - 1) == 0 and sections * own_object.size * 6 <= resident_bytes
    pieces, places = [], []
    if resident:
        height = side // members
        quarter = lax.dynamic_slice_in_dim(own_object, member * height, height, 1).astype(wire)
        direct = {}
        for distance in ([2,3,1]):
            swap = [(source, source ^ distance) for source in range(sections)]
            direct[distance] = lax.ppermute(quarter, "cuts", swap)
        for distance in sorted(direct):
            opposite = lax.ppermute(direct[distance], "probe", across)
            for piece, where in (
                (direct[distance], member),
                (opposite, (member + half_count) % members),
                (lax.ppermute(direct[distance], "probe", beside), member ^ 1),
                (lax.ppermute(opposite, "probe", beside), ((member ^ 1) + half_count) % members),
            ):
                pieces.append(piece)
                places += [own ^ distance, where * height]
    else:
        pieces.append(lax.all_gather(own_object.astype(wire), "cuts"))
    own_sums = sums_call(sections, positions, extent, side, len(pieces), resident)(
        scalars(own, half, *places), offsets, offsets_other, jnp.asarray(tables(extent)), own_object, probe,
        measured, measured_other, *pieces,
    )
    other_sums = lax.ppermute(own_sums, "probe", beside)
    summed = own_sums.astype(jnp.float32) + other_sums.astype(jnp.float32)
    updated = own_object - (step_size / (summed[2] + regular)) * summed[:2]
    return updated[:, None]


def solution(mesh):
    in_specs = (
        P(None, ("group", "cuts"), None, None),
        P("group", None, None),
        P(("group", "probe"), None, None),
        P(("group", "probe"), None),
    )
    out_specs = P(None, ("group", "cuts"), None, None)
    return jax.shard_map(
        on_device, mesh=mesh, in_specs=in_specs, out_specs=out_specs, check_vma=False
    )
```

time: 64.8 us -> 46 us (0.71)
  Pallas kernels: 29.9 us -> 11.4 us
    pallas_call x1, Pallas kernels: 29.9 us -> 11.4 us  [on_device(): sums_call(sections, positions, extent, side, len(pieces), resident)]
    unnamed x9 -> x7, local copies, waits for them, and re-layouts: 2.84 us -> 2.64 us
  transfers between devices with their start and end apart: 15 -> 15, of which waited for: 6 -> 7; matrix products, arithmetic and copies ran while one was open for 3% -> 4% of each run, Pallas kernels for 0% -> 0%
where the time goes in v2:
time: 46 us; the launch traced here: 45.7 us
  waiting for transfers between devices  15.5 us (34%)
  starting transfers between devices  12.3 us (27%)
  Pallas kernels  11.4 us (25%)
  local copies, waits for them, and re-layouts  3.81 us (8%)
  other arithmetic  2.56 us (6%)
    pallas_call x1, Pallas kernels, on_device(): sums_call(sections, positions, extent, side, len(pieces), resident)  11.4 us
    ppermute x3, starting transfers between devices, on_device(): direct[distance] = lax.ppermute(quarter, 'cuts', swap)  5.76 us
    ppermute x3, waiting for transfers between devices, on_device(): opposite = lax.ppermute(direct[distance], 'probe', across)  5.71 us
    ppermute x1, waiting for transfers between devices, on_device(): offsets_other = lax.ppermute(offsets, 'probe', across)  4.59 us
    ppermute x3, starting transfers between devices, on_device(): opposite = lax.ppermute(direct[distance], 'probe', across)  3.53 us
    unnamed x7, local copies, waits for them, and re-layouts  2.64 us
    ppermute x1, waiting for transfers between devices, on_device(): other_sums = lax.ppermute(own_sums, 'probe', beside)  2.15 us
    ppermute x3, waiting for transfers between devices, on_device(): direct[distance] = lax.ppermute(quarter, 'cuts', swap)  1.83 us
  transfers between devices with their start and end apart: 15, of which 7 were waited for; matrix products, arithmetic and copies ran while one was open for 4% of the time, Pallas kernels for 0%

profile of v2, /device:TPU:0, one launch (start us, length us, event | category | flops | bytes accessed | tf_op | source)
XLA Modules:
  0.0 45.7 jit_solution(15383580869287526459)
XLA Ops:
  0.0 1.1 %fusion.4 = bf16[2,96,384]{2,1,0:T(8,128)(2,1)S(1)} fusion(f32[2,1,384,384]{3,2,0,1:T(8,128)} %bitcast.20, s32[]{:T(128)S(6)} %select_n.29), kind=kLoop, calls=%fused_computation.8 | loop fusion | bytes 294916 | tf_op jit(solution)/shard_map/convert_element_type | solution.py:277
  1.1 5.1 %collective-permute-start.10 = (bf16[2,96,384]{2,1,0:T(8,128)(2,1)S(1)}, bf16[2,96,384]{2,1,0:T(8,128)(2,1)S(1)}, u32[]{:S(2)}, u32[]{:S(2)}) collective-permute-start(bf16[2,96,384]{2,1,0:T(8,128)(2,1)S(1)} %fusion.4), channel_id=1, source_target_pairs={{0,12},{4,8},{8,4},{12,0},{1,13},{5,9},{9,5},{13,1},{2,14},{6,10},... | collective-permute-start | bytes 442376 | tf_op jit(solution)/shard_map/ppermute | solution.py:281
  6.2 0.0 collective-permute-start.6
  6.2 0.6 %collective-permute-start.2 = (bf16[2,96,384]{2,1,0:T(8,128)(2,1)S(1)}, bf16[2,96,384]{2,1,0:T(8,128)(2,1)S(1)}, u32[]{:S(2)}, u32[]{:S(2)}) collective-permute-start(bf16[2,96,384]{2,1,0:T(8,128)(2,1)S(1)} %fusion.4), channel_id=1, source_target_pairs={{0,4},{4,0},{8,12},{12,8},{1,5},{5,1},{9,13},{13,9},{2,6},{6,2},{1... | collective-permute-start | bytes 442376 | tf_op jit(solution)/shard_map/ppermute | solution.py:281
  6.8 1.1 %convert_element_type.15.measured_own = bf16[8,128,128]{2,1,0:T(8,128)(2,1)S(1)} convert(f32[8,128,128]{2,1,0:T(8,128)} %param.7) | non-fusion elementwise | flops 131072 | bytes 786432 | tf_op jit(solution)/shard_map/convert_element_type | solution.py:269
  7.9 1.7 %collective-permute-start.1 = (bf16[8,128,128]{2,1,0:T(8,128)(2,1)S(1)}, bf16[8,128,128]{2,1,0:T(8,128)(2,1)S(1)}, u32[]{:S(2)}, u32[]{:S(2)}) collective-permute-start(bf16[8,128,128]{2,1,0:T(8,128)(2,1)S(1)} %convert_element_type.15.measured_own), channel_id=1, source_target_pairs={{0,2},{1,3},{2,0},{3,1},{4,6},{5,7},{6,4},{7,5},{8,10},{9,11},{10,... | collective-permute-start | bytes 786440 | tf_op jit(solution)/shard_map/ppermute | solution.py:270
  9.6 0.8 %copy.8.offsets_own_ref = s32[8,2]{1,0:T(8,128)S(1)} copy(s32[8,2]{0,1:T(2,128)} %param.8) | data formatting | bytes 128 | tf_op args[3]
  10.4 0.4 collective-permute-start
  10.8 0.2 collective-permute-done.10.rest_8_
  11.0 0.0 collective-permute-start.12
  11.0 4.6 %collective-permute-done.offsets_other_ref = s32[8,2]{1,0:T(8,128)S(1)} collective-permute-done((s32[8,2]{1,0:T(8,128)S(1)}, s32[8,2]{1,0:T(8,128)S(1)}, u32[]{:S(2)}, u32[]{:S(2)}) %collective-permute-start) | collective-permute-done | bytes 96 | tf_op jit(solution)/shard_map/ppermute | solution.py:271
  15.6 1.5 %collective-permute-start.11 = (bf16[2,96,384]{2,1,0:T(8,128)(2,1)S(1)}, bf16[2,96,384]{2,1,0:T(8,128)(2,1)S(1)}, u32[]{:S(2)}, u32[]{:S(2)}) collective-permute-start(bf16[2,96,384]{2,1,0:T(8,128)(2,1)S(1)} %collective-permute-done.10.rest_8_), channel_id=1, source_target_pairs={{0,2},{1,3},{2,0},{3,1},{4,6},{5,7},{6,4},{7,5},{8,10},{9,11},{10,... | collective-permute-start | bytes 442376 | tf_op jit(solution)/shard_map/ppermute | solution.py:283
  17.1 1.6 %collective-permute-done.6.rest_4_ = bf16[2,96,384]{2,1,0:T(8,128)(2,1)S(1)} collective-permute-done((bf16[2,96,384]{2,1,0:T(8,128)(2,1)S(1)}, bf16[2,96,384]{2,1,0:T(8,128)(2,1)S(1)}, u32[]{:S(2)}, u32[]{:S(2)}) %collective-permute-start.6) | collective-permute-done | bytes 147488 | tf_op jit(solution)/shard_map/ppermute | solution.py:281
  18.7 1.5 %collective-permute-start.7 = (bf16[2,96,384]{2,1,0:T(8,128)(2,1)S(1)}, bf16[2,96,384]{2,1,0:T(8,128)(2,1)S(1)}, u32[]{:S(2)}, u32[]{:S(2)}) collective-permute-start(bf16[2,96,384]{2,1,0:T(8,128)(2,1)S(1)} %collective-permute-done.6.rest_4_), channel_id=1, source_target_pairs={{0,2},{1,3},{2,0},{3,1},{4,6},{5,7},{6,4},{7,5},{8,10},{9,11},{10,... | collective-permute-start | bytes 442376 | tf_op jit(solution)/shard_map/ppermute | solution.py:283
  20.2 0.5 %collective-permute-start.3 = (bf16[2,96,384]{2,1,0:T(8,128)(2,1)S(1)}, bf16[2,96,384]{2,1,0:T(8,128)(2,1)S(1)}, u32[]{:S(2)}, u32[]{:S(2)}) collective-permute-start(bf16[2,96,384]{2,1,0:T(8,128)(2,1)S(1)} %collective-permute-done.2.rest_0_), channel_id=1, source_target_pairs={{0,2},{1,3},{2,0},{3,1},{4,6},{5,7},{6,4},{7,5},{8,10},{9,11},{10,... | collective-permute-start | bytes 442376 | tf_op jit(solution)/shard_map/ppermute | solution.py:283
  20.7 0.0 collective-permute-start.8
  20.7 0.0 collective-permute-done.12.rest_10_
  20.7 0.5 %collective-permute-start.4 = (bf16[2,96,384]{2,1,0:T(8,128)(2,1)S(1)}, bf16[2,96,384]{2,1,0:T(8,128)(2,1)S(1)}, u32[]{:S(2)}, u32[]{:S(2)}) collective-permute-start(bf16[2,96,384]{2,1,0:T(8,128)(2,1)S(1)} %collective-permute-done.2.rest_0_), channel_id=1, source_target_pairs={{0,1},{1,0},{2,3},{3,2},{4,5},{5,4},{6,7},{7,6},{8,9},{9,8},{10,11... | collective-permute-start | bytes 442376 | tf_op jit(solution)/shard_map/ppermute | solution.py:287
  21.2 0.1 collective-permute-start.13
  21.3 4.1 %collective-permute-done.7.rest_5_ = bf16[2,96,384]{2,1,0:T(8,128)(2,1)S(1)} collective-permute-done((bf16[2,96,384]{2,1,0:T(8,128)(2,1)S(1)}, bf16[2,96,384]{2,1,0:T(8,128)(2,1)S(1)}, u32[]{:S(2)}, u32[]{:S(2)}) %collective-permute-start.7) | collective-permute-done | bytes 147488 | tf_op jit(solution)/shard_map/ppermute | solution.py:283
  25.4 0.0 collective-permute-start.9
  25.5 1.6 %collective-permute-done.3.rest_1_ = bf16[2,96,384]{2,1,0:T(8,128)(2,1)S(1)} collective-permute-done((bf16[2,96,384]{2,1,0:T(8,128)(2,1)S(1)}, bf16[2,96,384]{2,1,0:T(8,128)(2,1)S(1)}, u32[]{:S(2)}, u32[]{:S(2)}) %collective-permute-start.3) | collective-permute-done | bytes 147488 | tf_op jit(solution)/shard_map/ppermute | solution.py:283
  27.0 0.1 stack.56.place_ref
  27.2 1.2 %collective-permute-done.5.rest_3_ = bf16[2,96,384]{2,1,0:T(8,128)(2,1)S(1)} collective-permute-done((bf16[2,96,384]{2,1,0:T(8,128)(2,1)S(1)}, bf16[2,96,384]{2,1,0:T(8,128)(2,1)S(1)}, u32[]{:S(2)}, u32[]{:S(2)}) %collective-permute-start.5) | collective-permute-done | bytes 147488 | tf_op jit(solution)/shard_map/ppermute | solution.py:288
  28.4 1.0 %copy-done.1 = bf16[4,256,256]{2,1,0:T(8,128)(2,1)S(1)} copy-done((bf16[4,256,256]{2,1,0:T(8,128)(2,1)S(1)}, bf16[4,256,256]{2,1,0:T(8,128)(2,1)}, u32[]{:S(2)}) %copy-start.1) | copy-done | bytes 524312
  29.4 0.8 %copy-done.2 = bf16[2,128,128]{2,1,0:T(8,128)(2,1)S(1)} copy-done((bf16[2,128,128]{2,1,0:T(8,128)(2,1)S(1)}, bf16[2,128,128]{2,1,0:T(8,128)(2,1)}, u32[]{:S(2)}) %copy-start.2) | copy-done | bytes 65560
  30.3 11.4 %shard_map.55 = bf16[3,384,384]{2,1,0:T(8,128)(2,1)S(1)} custom-call(s32[26]{0:T(128)S(1)} %stack.56.place_ref, s32[8,2]{1,0:T(8,128)S(1)} %copy.8.offsets_own_ref, s32[8,2]{1,0:T(8,128)S(1)} %collective-permute-done.offsets_other_ref, bf16[4,256,256]{2,1,0:T(8,128)(2,1)S(1)} %copy-done.1, f32[2,384,384]{2,1,0:T(8,128)S(1)} %bitcast.21, ...), custom_call_target="tpu_custom_call" | custom-call | tf_op jit(solution)/shard_map/pallas_call | solution.py:294
  41.7 0.3 collective-permute-start.14
  42.0 2.2 %collective-permute-done.14 = bf16[3,384,384]{2,1,0:T(8,128)(2,1)S(1)} collective-permute-done((bf16[3,384,384]{2,1,0:T(8,128)(2,1)S(1)}, bf16[3,384,384]{2,1,0:T(8,128)(2,1)S(1)}, u32[]{:S(2)}, u32[]{:S(2)}) %collective-permute-start.14) | collective-permute-done | bytes 884768 | tf_op jit(solution)/shard_map/ppermute | solution.py:298
  44.2 0.2 convert_add_fusion
  44.4 0.1 fusion.3
  44.4 1.2 %fusion.1 = f32[2,1,384,384]{3,2,1,0:T(8,128)} fusion(f32[3,384,384]{2,1,0:T(8,128)S(1)} %convert_add_fusion, f32[384,384]{1,0:T(8,128)S(1)} %fusion.3, f32[2,1,384,384]{3,2,1,0:T(8,128)S(1)} %copy-done), kind=kLoop, calls=%fused_computation.3 | loop fusion | flops 589824 | bytes 4128768 | tf_op jit(solution)/shard_map/broadcast_in_dim | solution.py:301
  (12 shorter events, 0.0 us)
Async XLA Ops:
  0.0 28.4 %copy-start = (f32[2,1,384,384]{3,2,1,0:T(8,128)S(1)}, f32[2,1,384,384]{3,2,1,0:T(8,128)}, u32[]{:S(2)}) copy-start(f32[2,1,384,384]{3,2,1,0:T(8,128)} %param.5) | copy-start | bytes 3538948
  1.1 9.9 %collective-permute-start.10 = (bf16[2,96,384]{2,1,0:T(8,128)(2,1)S(1)}, bf16[2,96,384]{2,1,0:T(8,128)(2,1)S(1)}, u32[]{:S(2)}, u32[]{:S(2)}) collective-permute-start(bf16[2,96,384]{2,1,0:T(8,128)(2,1)S(1)} %fusion.4), channel_id=1, source_target_pairs={{0,12},{4,8},{8,4},{12,0},{1,13},{5,9},{9,5},{13,1},{2,14},{6,10},... | collective-permute-start | bytes 442376 | tf_op jit(solution)/shard_map/ppermute | solution.py:281
  6.2 12.5 %collective-permute-start.6 = (bf16[2,96,384]{2,1,0:T(8,128)(2,1)S(1)}, bf16[2,96,384]{2,1,0:T(8,128)(2,1)S(1)}, u32[]{:S(2)}, u32[]{:S(2)}) collective-permute-start(bf16[2,96,384]{2,1,0:T(8,128)(2,1)S(1)} %fusion.4), channel_id=1, source_target_pairs={{0,8},{4,12},{8,0},{12,4},{1,9},{5,13},{9,1},{13,5},{2,10},{6,14},... | collective-permute-start | bytes 442376 | tf_op jit(solution)/shard_map/ppermute | solution.py:281
  6.2 14.0 %collective-permute-start.2 = (bf16[2,96,384]{2,1,0:T(8,128)(2,1)S(1)}, bf16[2,96,384]{2,1,0:T(8,128)(2,1)S(1)}, u32[]{:S(2)}, u32[]{:S(2)}) collective-permute-start(bf16[2,96,384]{2,1,0:T(8,128)(2,1)S(1)} %fusion.4), channel_id=1, source_target_pairs={{0,4},{4,0},{8,12},{12,8},{1,5},{5,1},{9,13},{13,9},{2,6},{6,2},{1... | collective-permute-start | bytes 442376 | tf_op jit(solution)/shard_map/ppermute | solution.py:281
  7.9 12.8 %collective-permute-start.1 = (bf16[8,128,128]{2,1,0:T(8,128)(2,1)S(1)}, bf16[8,128,128]{2,1,0:T(8,128)(2,1)S(1)}, u32[]{:S(2)}, u32[]{:S(2)}) collective-permute-start(bf16[8,128,128]{2,1,0:T(8,128)(2,1)S(1)} %convert_element_type.15.measured_own), channel_id=1, source_target_pairs={{0,2},{1,3},{2,0},{3,1},{4,6},{5,7},{6,4},{7,5},{8,10},{9,11},{10,... | collective-permute-start | bytes 786440 | tf_op jit(solution)/shard_map/ppermute | solution.py:270
  10.4 5.2 %collective-permute-start = (s32[8,2]{1,0:T(8,128)S(1)}, s32[8,2]{1,0:T(8,128)S(1)}, u32[]{:S(2)}, u32[]{:S(2)}) collective-permute-start(s32[8,2]{1,0:T(8,128)S(1)} %copy.8.offsets_own_ref), channel_id=1, source_target_pairs={{0,2},{1,3},{2,0},{3,1},{4,6},{5,7},{6,4},{7,5},{8,10},{9,11},{10,... | collective-permute-start | bytes 200 | tf_op jit(solution)/shard_map/ppermute | solution.py:271
  11.0 9.8 %collective-permute-start.12 = (bf16[2,96,384]{2,1,0:T(8,128)(2,1)S(1)}, bf16[2,96,384]{2,1,0:T(8,128)(2,1)S(1)}, u32[]{:S(2)}, u32[]{:S(2)}) collective-permute-start(bf16[2,96,384]{2,1,0:T(8,128)(2,1)S(1)} %collective-permute-done.10.rest_8_), channel_id=1, source_target_pairs={{0,1},{1,0},{2,3},{3,2},{4,5},{5,4},{6,7},{7,6},{8,9},{9,8},{10,11... | collective-permute-start | bytes 442376 | tf_op jit(solution)/shard_map/ppermute | solution.py:287
  15.6 5.7 %collective-permute-start.11 = (bf16[2,96,384]{2,1,0:T(8,128)(2,1)S(1)}, bf16[2,96,384]{2,1,0:T(8,128)(2,1)S(1)}, u32[]{:S(2)}, u32[]{:S(2)}) collective-permute-start(bf16[2,96,384]{2,1,0:T(8,128)(2,1)S(1)} %collective-permute-done.10.rest_8_), channel_id=1, source_target_pairs={{0,2},{1,3},{2,0},{3,1},{4,6},{5,7},{6,4},{7,5},{8,10},{9,11},{10,... | collective-permute-start | bytes 442376 | tf_op jit(solution)/shard_map/ppermute | solution.py:283
  18.7 6.8 %collective-permute-start.7 = (bf16[2,96,384]{2,1,0:T(8,128)(2,1)S(1)}, bf16[2,96,384]{2,1,0:T(8,128)(2,1)S(1)}, u32[]{:S(2)}, u32[]{:S(2)}) collective-permute-start(bf16[2,96,384]{2,1,0:T(8,128)(2,1)S(1)} %collective-permute-done.6.rest_4_), channel_id=1, source_target_pairs={{0,2},{1,3},{2,0},{3,1},{4,6},{5,7},{6,4},{7,5},{8,10},{9,11},{10,... | collective-permute-start | bytes 442376 | tf_op jit(solution)/shard_map/ppermute | solution.py:283
  20.2 6.9 %collective-permute-start.3 = (bf16[2,96,384]{2,1,0:T(8,128)(2,1)S(1)}, bf16[2,96,384]{2,1,0:T(8,128)(2,1)S(1)}, u32[]{:S(2)}, u32[]{:S(2)}) collective-permute-start(bf16[2,96,384]{2,1,0:T(8,128)(2,1)S(1)} %collective-permute-done.2.rest_0_), channel_id=1, source_target_pairs={{0,2},{1,3},{2,0},{3,1},{4,6},{5,7},{6,4},{7,5},{8,10},{9,11},{10,... | collective-permute-start | bytes 442376 | tf_op jit(solution)/shard_map/ppermute | solution.py:283
  20.7 6.4 %collective-permute-start.8 = (bf16[2,96,384]{2,1,0:T(8,128)(2,1)S(1)}, bf16[2,96,384]{2,1,0:T(8,128)(2,1)S(1)}, u32[]{:S(2)}, u32[]{:S(2)}) collective-permute-start(bf16[2,96,384]{2,1,0:T(8,128)(2,1)S(1)} %collective-permute-done.6.rest_4_), channel_id=1, source_target_pairs={{0,1},{1,0},{2,3},{3,2},{4,5},{5,4},{6,7},{7,6},{8,9},{9,8},{10,11... | collective-permute-start | bytes 442376 | tf_op jit(solution)/shard_map/ppermute | solution.py:287
  20.7 6.4 %collective-permute-start.4 = (bf16[2,96,384]{2,1,0:T(8,128)(2,1)S(1)}, bf16[2,96,384]{2,1,0:T(8,128)(2,1)S(1)}, u32[]{:S(2)}, u32[]{:S(2)}) collective-permute-start(bf16[2,96,384]{2,1,0:T(8,128)(2,1)S(1)} %collective-permute-done.2.rest_0_), channel_id=1, source_target_pairs={{0,1},{1,0},{2,3},{3,2},{4,5},{5,4},{6,7},{7,6},{8,9},{9,8},{10,11... | collective-permute-start | bytes 442376 | tf_op jit(solution)/shard_map/ppermute | solution.py:287
  21.2 5.9 %collective-permute-start.13 = (bf16[2,96,384]{2,1,0:T(8,128)(2,1)S(1)}, bf16[2,96,384]{2,1,0:T(8,128)(2,1)S(1)}, u32[]{:S(2)}, u32[]{:S(2)}) collective-permute-start(bf16[2,96,384]{2,1,0:T(8,128)(2,1)S(1)} %collective-permute-done.11.rest_9_), channel_id=1, source_target_pairs={{0,1},{1,0},{2,3},{3,2},{4,5},{5,4},{6,7},{7,6},{8,9},{9,8},{10,11... | collective-permute-start | bytes 442376 | tf_op jit(solution)/shard_map/ppermute | solution.py:288
  25.4 1.7 %collective-permute-start.9 = (bf16[2,96,384]{2,1,0:T(8,128)(2,1)S(1)}, bf16[2,96,384]{2,1,0:T(8,128)(2,1)S(1)}, u32[]{:S(2)}, u32[]{:S(2)}) collective-permute-start(bf16[2,96,384]{2,1,0:T(8,128)(2,1)S(1)} %collective-permute-done.7.rest_5_), channel_id=1, source_target_pairs={{0,1},{1,0},{2,3},{3,2},{4,5},{5,4},{6,7},{7,6},{8,9},{9,8},{10,11... | collective-permute-start | bytes 442376 | tf_op jit(solution)/shard_map/ppermute | solution.py:288
  27.0 1.4 %collective-permute-start.5 = (bf16[2,96,384]{2,1,0:T(8,128)(2,1)S(1)}, bf16[2,96,384]{2,1,0:T(8,128)(2,1)S(1)}, u32[]{:S(2)}, u32[]{:S(2)}) collective-permute-start(bf16[2,96,384]{2,1,0:T(8,128)(2,1)S(1)} %collective-permute-done.3.rest_1_), channel_id=1, source_target_pairs={{0,1},{1,0},{2,3},{3,2},{4,5},{5,4},{6,7},{7,6},{8,9},{9,8},{10,11... | collective-permute-start | bytes 442376 | tf_op jit(solution)/shard_map/ppermute | solution.py:288
  28.4 1.0 %copy-start.1 = (bf16[4,256,256]{2,1,0:T(8,128)(2,1)S(1)}, bf16[4,256,256]{2,1,0:T(8,128)(2,1)}, u32[]{:S(2)}) copy-start(bf16[4,256,256]{2,1,0:T(8,128)(2,1)} %constant.60.clone.tables_hbm) | copy-start | bytes 1572868
  29.4 0.8 %copy-start.2 = (bf16[2,128,128]{2,1,0:T(8,128)(2,1)S(1)}, bf16[2,128,128]{2,1,0:T(8,128)(2,1)}, u32[]{:S(2)}) copy-start(bf16[2,128,128]{2,1,0:T(8,128)(2,1)} %probe_ref.1) | copy-start | bytes 196612
  41.7 2.5 %collective-permute-start.14 = (bf16[3,384,384]{2,1,0:T(8,128)(2,1)S(1)}, bf16[3,384,384]{2,1,0:T(8,128)(2,1)S(1)}, u32[]{:S(2)}, u32[]{:S(2)}) collective-permute-start(bf16[3,384,384]{2,1,0:T(8,128)(2,1)S(1)} %shard_map.55), channel_id=1, source_target_pairs={{0,1},{1,0},{2,3},{3,2},{4,5},{5,4},{6,7},{7,6},{8,9},{9,8},{10,11... | collective-permute-start | bytes 2654216 | tf_op jit(solution)/shard_map/ppermute | solution.py:298

commit v3 on v2

--- a/solution.py
+++ b/solution.py
@@ -36,11 +36,10 @@
     )
 
 
-def corner_of(half, positions, blocks, offsets_own_ref, offsets_other_ref, position):
-    is_own = position // positions == half
+def corner_of(half, positions, blocks, offsets_ref, position):
+    source = (position // positions != half).astype(jnp.int32)
     slot = lax.rem(position, positions)
-    row = jnp.where(is_own, offsets_own_ref[slot, 0], offsets_other_ref[slot, 0])
-    column = jnp.where(is_own, offsets_own_ref[slot, 1], offsets_other_ref[slot, 1])
+    row, column = offsets_ref[source, slot, 0], offsets_ref[source, slot, 1]
     first = column // lanes
     return row, first, jnp.minimum(first + 1, blocks - 1), column - first * lanes
 
@@ -113,21 +112,32 @@
 
 def sums_kernel(
     sections, pieces, resident, group, batch,
-    place_ref, offsets_own_ref, offsets_other_ref, tables_hbm, object_hbm, probe_ref, measured_own, measured_other, *rest,
+    place_ref, tables_hbm, object_hbm, probe_hbm, measured_own, measured_other, *rest,
 ):
     piece_refs = rest[:pieces]
-    out_ref, field, waves, sums, table_ref, own_ref, sems = rest[pieces:]
+    out_ref, field, waves, sums, table_ref, own_ref, probe_ref, numbers, offsets_ref, sems = rest[pieces:]
     own, half = place_ref[0], place_ref[1]
     total, extent = waves.shape[1], waves.shape[3]
     positions = total // 2
     blocks = sums.shape[1]
-    corners = functools.partial(corner_of, half, positions, blocks, offsets_own_ref, offsets_other_ref)
-
+    corners = functools.partial(corner_of, half, positions, blocks, offsets_ref)
+
+    for source, measured in enumerate((measured_own, measured_other)):
+        numbers[source] = measured[positions, :numbers.shape[1]].astype(jnp.float32).astype(jnp.int32)
+    offsets_copy = pltpu.make_async_copy(numbers, offsets_ref, sems.at[3])
+    offsets_copy.start()
+
+    probe_copy = pltpu.make_async_copy(probe_hbm, probe_ref, sems.at[2])
+    probe_copy.start()
     table_copy = pltpu.make_async_copy(tables_hbm, table_ref, sems.at[0])
     table_copy.start()
     if resident:
         own_copy = pltpu.make_async_copy(object_hbm, own_ref, sems.at[1])
         own_copy.start()
+        place_pieces(field, place_ref, 2, piece_refs)
+    sums[...] = jnp.zeros_like(sums)
+    probe_copy.wait()
+    offsets_copy.wait()
 
     def start_wave(position, carry):
         shift = corners(position)[3]
@@ -136,9 +146,7 @@
         return carry
 
     lax.fori_loop(0, total, start_wave, 0, unroll=4)
-    sums[...] = jnp.zeros_like(sums)
     if resident:
-        place_pieces(field, place_ref, 2, piece_refs)
         own_copy.wait()
         for part in range(2):
             for block in range(blocks):
@@ -224,6 +232,7 @@
 smem = pl.BlockSpec(memory_space=pltpu.SMEM)
 vmem = pl.BlockSpec(memory_space=pltpu.VMEM)
 anywhere = pl.BlockSpec(memory_space=pl.ANY)
+hbm = pl.BlockSpec(memory_space=pltpu.HBM)
 GROUP, BATCH = 16, 16
 
 
@@ -234,7 +243,7 @@
     return pl.pallas_call(
         functools.partial(sums_kernel, sections, pieces, resident, group, math.gcd(BATCH, group)),
         out_shape=jax.ShapeDtypeStruct((3, side, side), wire),
-        in_specs=[smem] * 3 + [anywhere] * 2 + [vmem] * 3 + [vmem if resident else anywhere] * pieces,
+        in_specs=[smem] + [hbm] * 3 + [vmem] * 2 + [vmem if resident else anywhere] * pieces,
         out_specs=vmem,
         scratch_shapes=[
             pltpu.VMEM((sections if resident else 1,) + slice_shape, jnp.float32),
@@ -242,7 +251,10 @@
             pltpu.VMEM((3,) + slice_shape[1:], jnp.float32),
             pltpu.VMEM((4, 2 * extent, 2 * extent), jnp.bfloat16),
             pltpu.VMEM((2, side, side), jnp.float32 if resident else wire),
-            pltpu.SemaphoreType.DMA((2,)),
+            pltpu.VMEM((2, extent, extent), jnp.bfloat16),
+            pltpu.VMEM((2, -(-positions // 16) * 16, extent), jnp.int32),
+            pltpu.SMEM((2, -(-positions // 16) * 16, extent), jnp.int32),
+            pltpu.SemaphoreType.DMA((4,)),
         ],
         compiler_params=pltpu.CompilerParams(vmem_limit_bytes=40 * 2**20),
     )
@@ -266,33 +278,36 @@
     def scalars(*values):
         return jnp.stack([jnp.asarray(value, jnp.int32) for value in values])
 
-    measured = intensities.astype(wire)
+    plane = jnp.pad(offsets.astype(wire), ((0, extent - positions), (0, extent - offsets.shape[1])))
+    measured = jnp.concatenate([intensities.astype(wire), plane[None]])
     measured_other = lax.ppermute(measured, "probe", across)
-    offsets_other = lax.ppermute(offsets, "probe", across)
 
     resident = sections & (sections - 1) == 0 and sections * own_object.size * 6 <= resident_bytes
     pieces, places = [], []
     if resident:
         height = side // members
         quarter = lax.dynamic_slice_in_dim(own_object, member * height, height, 1).astype(wire)
-        direct = {}
-        for distance in ([2,3,1]):
-            swap = [(source, source ^ distance) for source in range(sections)]
-            direct[distance] = lax.ppermute(quarter, "cuts", swap)
-        for distance in sorted(direct):
-            opposite = lax.ppermute(direct[distance], "probe", across)
+        swap = lambda distance: [(source, source ^ distance) for source in range(sections)]
+        go = lambda value, distance: lax.ppermute(value, "cuts", swap(distance))
+        over = lambda value: lax.ppermute(value, "probe", across)
+        direct = {2: go(quarter, 2), 1: go(quarter, 1)}
+        direct[1], measured_other = lax.optimization_barrier((direct[1], measured_other))
+        direct[3] = go(direct[2], 1)
+        opposite = {distance: over(direct[distance]) for distance in (2, 1)}
+        opposite[3] = go(opposite[2], 1)
+        for distance in (2, 1, 3):
             for piece, where in (
                 (direct[distance], member),
-                (opposite, (member + half_count) % members),
+                (opposite[distance], (member + half_count) % members),
                 (lax.ppermute(direct[distance], "probe", beside), member ^ 1),
-                (lax.ppermute(opposite, "probe", beside), ((member ^ 1) + half_count) % members),
+                (lax.ppermute(opposite[distance], "probe", beside), ((member ^ 1) + half_count) % members),
             ):
                 pieces.append(piece)
                 places += [own ^ distance, where * height]
     else:
         pieces.append(lax.all_gather(own_object.astype(wire), "cuts"))
     own_sums = sums_call(sections, positions, extent, side, len(pieces), resident)(
-        scalars(own, half, *places), offsets, offsets_other, jnp.asarray(tables(extent)), own_object, probe,
+        scalars(own, half, *places), jnp.asarray(tables(extent)), own_object, probe,
         measured, measured_other, *pieces,
     )
     other_sums = lax.ppermute(own_sums, "probe", beside)

time: 46 us -> 43.7 us (0.950)
  local copies, waits for them, and re-layouts: 3.81 us -> 0.24 us
  waiting for transfers between devices: 15.5 us -> 16.8 us
  starting transfers between devices: 12.3 us -> 11.1 us
  other arithmetic: 2.56 us -> 3.38 us
  Pallas kernels: 11.4 us -> 11.9 us
    unnamed x7 -> x6, local copies, waits for them, and re-layouts: 2.64 us -> 0.01 us
    ppermute x10 -> x9, starting transfers between devices: 9.75 us -> 7.58 us  [the longest x4 6.04 us: on_device(): go = lambda value, distance: lax.ppermute(value, 'cuts', swap(distance))]
    ppermute x10 -> x9, waiting for transfers between devices: 13.4 us -> 14.7 us  [the longest x4 8.13 us: on_device(): go = lambda value, distance: lax.ppermute(value, 'cuts', swap(distance))]
    ppermute x1, starting transfers between devices: 1.7 us -> 3.01 us  [on_device(): measured_other = lax.ppermute(measured, 'probe', across)]
    convert_element_type x1, local copies, waits for them, and re-layouts: 1.08 us -> 0.02 us  [on_device(): lax.dynamic_slice_in_dim(own_object, member * height, height, 1)]
    convert_element_type x1 -> x2, other arithmetic: 1.08 us -> 1.89 us  [the longest x1 1.08 us: on_device(): measured = jnp.concatenate([intensities.astype(wire), plane[None]])]
    pallas_call x1, Pallas kernels: 11.4 us -> 11.9 us  [on_device(): sums_call(sections, positions, extent, side, len(pieces), resident)]
  transfers between devices with their start and end apart: 15 -> 14, of which waited for: 7 -> 7; matrix products, arithmetic and copies ran while one was open for 4% -> 0% of each run, Pallas kernels for 0% -> 0%
where the time goes in v3:
time: 43.7 us; the launch traced here: 43.5 us
  waiting for transfers between devices  16.8 us (38%)
  Pallas kernels  11.9 us (27%)
  starting transfers between devices  11.1 us (25%)
  other arithmetic  3.38 us (8%)
    pallas_call x1, Pallas kernels, on_device(): sums_call(sections, positions, extent, side, len(pieces), resident)  11.9 us
    ppermute x4, waiting for transfers between devices, on_device(): go = lambda value, distance: lax.ppermute(value, 'cuts', swap(distance))  8.13 us
    ppermute x4, starting transfers between devices, on_device(): go = lambda value, distance: lax.ppermute(value, 'cuts', swap(distance))  6.04 us
    ppermute x2, waiting for transfers between devices, on_device(): over = lambda value: lax.ppermute(value, 'probe', across)  5.22 us
    ppermute x1, starting transfers between devices, on_device(): measured_other = lax.ppermute(measured, 'probe', across)  3.01 us
    ppermute x1, waiting for transfers between devices, on_device(): other_sums = lax.ppermute(own_sums, 'probe', beside)  2.05 us
    ppermute x3, waiting for transfers between devices, on_device(): lax.ppermute(opposite[distance], 'probe', beside)  1.37 us
    broadcast_in_dim x1, other arithmetic, on_device(): return updated[:, None]  1.2 us
  transfers between devices with their start and end apart: 14, of which 7 were waited for; matrix products, arithmetic and copies ran while one was open for 0% of the time, Pallas kernels for 0%

profile of v3, /device:TPU:0, one launch (start us, length us, event | category | flops | bytes accessed | tf_op | source)
XLA Modules:
  0.0 43.5 jit_solution(2465263664740677411)
XLA Ops:
  0.0 0.8 %convert_element_type.21 = bf16[8,2]{0,1:T(2,128)(2,1)S(1)} convert(s32[8,2]{0,1:T(2,128)} %param.8) | non-fusion elementwise | flops 16 | bytes 96 | tf_op jit(solution)/shard_map/convert_element_type | solution.py:281
  0.8 0.1 copy.9
  0.9 1.1 %convert_element_type.20 = bf16[8,128,128]{2,1,0:T(8,128)(2,1)S(1)} convert(f32[8,128,128]{2,1,0:T(8,128)} %param.7) | non-fusion elementwise | flops 131072 | bytes 786432 | tf_op jit(solution)/shard_map/convert_element_type | solution.py:282
  2.0 3.0 %collective-permute-start.1 = (bf16[9,128,128]{2,1,0:T(8,128)(2,1)S(1)}, bf16[9,128,128]{2,1,0:T(8,128)(2,1)S(1)}, u32[]{:S(2)}, u32[]{:S(2)}) collective-permute-start(bf16[9,128,128]{2,1,0:T(8,128)(2,1)S(1)} %pad_maximum_fusion.measured_own), channel_id=1, source_target_pairs={{0,2},{1,3},{2,0},{3,1},{4,6},{5,7},{6,4},{7,5},{8,10},{9,11},{10,... | collective-permute-start | bytes 884744 | tf_op jit(solution)/shard_map/ppermute | solution.py:283
  5.1 2.7 %collective-permute-start.2 = (bf16[2,96,384]{2,1,0:T(8,128)(2,1)S(1)}, bf16[2,96,384]{2,1,0:T(8,128)(2,1)S(1)}, u32[]{:S(2)}, u32[]{:S(2)}) collective-permute-start(bf16[2,96,384]{2,1,0:T(8,128)(2,1)S(1)} %fusion.4), channel_id=1, source_target_pairs={{0,8},{4,12},{8,0},{12,4},{1,9},{5,13},{9,1},{13,5},{2,10},{6,14},... | collective-permute-start | bytes 442376 | tf_op jit(solution)/shard_map/ppermute | solution.py:291
  7.7 1.6 %collective-permute-start = (bf16[2,96,384]{2,1,0:T(8,128)(2,1)S(1)}, bf16[2,96,384]{2,1,0:T(8,128)(2,1)S(1)}, u32[]{:S(2)}, u32[]{:S(2)}) collective-permute-start(bf16[2,96,384]{2,1,0:T(8,128)(2,1)S(1)} %fusion.4), channel_id=1, source_target_pairs={{0,4},{4,0},{8,12},{12,8},{1,5},{5,1},{9,13},{13,9},{2,6},{6,2},{1... | collective-permute-start | bytes 442376 | tf_op jit(solution)/shard_map/ppermute | solution.py:291
  9.3 5.3 %collective-permute-done.2.rest_0_ = bf16[2,96,384]{2,1,0:T(8,128)(2,1)S(1)} collective-permute-done((bf16[2,96,384]{2,1,0:T(8,128)(2,1)S(1)}, bf16[2,96,384]{2,1,0:T(8,128)(2,1)S(1)}, u32[]{:S(2)}, u32[]{:S(2)}) %collective-permute-start.2) | collective-permute-done | bytes 147488 | tf_op jit(solution)/shard_map/ppermute | solution.py:291
  14.6 0.5 %collective-permute-start.3 = (bf16[2,96,384]{2,1,0:T(8,128)(2,1)S(1)}, bf16[2,96,384]{2,1,0:T(8,128)(2,1)S(1)}, u32[]{:S(2)}, u32[]{:S(2)}) collective-permute-start(bf16[2,96,384]{2,1,0:T(8,128)(2,1)S(1)} %collective-permute-done.2.rest_0_), channel_id=1, source_target_pairs={{0,2},{1,3},{2,0},{3,1},{4,6},{5,7},{6,4},{7,5},{8,10},{9,11},{10,... | collective-permute-start | bytes 442376 | tf_op jit(solution)/shard_map/ppermute | solution.py:292
  15.1 0.6 %collective-permute-start.9 = (bf16[2,96,384]{2,1,0:T(8,128)(2,1)S(1)}, bf16[2,96,384]{2,1,0:T(8,128)(2,1)S(1)}, u32[]{:S(2)}, u32[]{:S(2)}) collective-permute-start(bf16[2,96,384]{2,1,0:T(8,128)(2,1)S(1)} %collective-permute-done.2.rest_0_), channel_id=1, source_target_pairs={{0,4},{4,0},{8,12},{12,8},{1,5},{5,1},{9,13},{13,9},{2,6},{6,2},{1... | collective-permute-start | bytes 442376 | tf_op jit(solution)/shard_map/ppermute | solution.py:291
  15.7 0.0 collective-permute-start.4
  15.7 0.0 collective-permute-done.rest_4_
  15.7 0.0 collective-permute-done.1.measured_other
  15.7 4.0 %collective-permute-done.3.rest_1_ = bf16[2,96,384]{2,1,0:T(8,128)(2,1)S(1)} collective-permute-done((bf16[2,96,384]{2,1,0:T(8,128)(2,1)S(1)}, bf16[2,96,384]{2,1,0:T(8,128)(2,1)S(1)}, u32[]{:S(2)}, u32[]{:S(2)}) %collective-permute-start.3) | collective-permute-done | bytes 147488 | tf_op jit(solution)/shard_map/ppermute | solution.py:292
  19.8 1.2 %collective-permute-start.10 = (bf16[2,96,384]{2,1,0:T(8,128)(2,1)S(1)}, bf16[2,96,384]{2,1,0:T(8,128)(2,1)S(1)}, u32[]{:S(2)}, u32[]{:S(2)}) collective-permute-start(bf16[2,96,384]{2,1,0:T(8,128)(2,1)S(1)} %collective-permute-done.3.rest_1_), channel_id=1, source_target_pairs={{0,4},{4,0},{8,12},{12,8},{1,5},{5,1},{9,13},{13,9},{2,6},{6,2},{1... | collective-permute-start | bytes 442376 | tf_op jit(solution)/shard_map/ppermute | solution.py:291
  21.0 0.5 %collective-permute-start.6 = (bf16[2,96,384]{2,1,0:T(8,128)(2,1)S(1)}, bf16[2,96,384]{2,1,0:T(8,128)(2,1)S(1)}, u32[]{:S(2)}, u32[]{:S(2)}) collective-permute-start(bf16[2,96,384]{2,1,0:T(8,128)(2,1)S(1)} %collective-permute-done.rest_4_), channel_id=1, source_target_pairs={{0,2},{1,3},{2,0},{3,1},{4,6},{5,7},{6,4},{7,5},{8,10},{9,11},{10,... | collective-permute-start | bytes 442376 | tf_op jit(solution)/shard_map/ppermute | solution.py:292
  21.5 0.0 collective-permute-start.7
  21.5 0.0 collective-permute-done.9.rest_8_
  21.5 0.5 %collective-permute-start.5 = (bf16[2,96,384]{2,1,0:T(8,128)(2,1)S(1)}, bf16[2,96,384]{2,1,0:T(8,128)(2,1)}, u32[]{:S(2)}, u32[]{:S(2)}) collective-permute-start(bf16[2,96,384]{2,1,0:T(8,128)(2,1)S(1)} %collective-permute-done.3.rest_1_), channel_id=1, source_target_pairs={{0,1},{1,0},{2,3},{3,2},{4,5},{5,4},{6,7},{7,6},{8,9},{9,8},{10,11... | collective-permute-start | bytes 442376 | tf_op jit(solution)/shard_map/ppermute | solution.py:303
  22.0 0.0 collective-permute-done.4.rest_2_
  22.0 0.1 collective-permute-start.11
  22.1 2.8 %collective-permute-done.10.rest_9_ = bf16[2,96,384]{2,1,0:T(8,128)(2,1)S(1)} collective-permute-done((bf16[2,96,384]{2,1,0:T(8,128)(2,1)S(1)}, bf16[2,96,384]{2,1,0:T(8,128)(2,1)S(1)}, u32[]{:S(2)}, u32[]{:S(2)}) %collective-permute-start.10) | collective-permute-done | bytes 147488 | tf_op jit(solution)/shard_map/ppermute | solution.py:291
  24.9 1.2 %collective-permute-done.6.rest_5_ = bf16[2,96,384]{2,1,0:T(8,128)(2,1)S(1)} collective-permute-done((bf16[2,96,384]{2,1,0:T(8,128)(2,1)S(1)}, bf16[2,96,384]{2,1,0:T(8,128)(2,1)S(1)}, u32[]{:S(2)}, u32[]{:S(2)}) %collective-permute-start.6) | collective-permute-done | bytes 147488 | tf_op jit(solution)/shard_map/ppermute | solution.py:292
  26.1 0.0 collective-permute-start.8
  26.1 0.1 stack.56.place_ref
  26.2 0.2 collective-permute-done.12.rest_11_
  26.4 1.2 %collective-permute-done.8.rest_7_ = bf16[2,96,384]{2,1,0:T(8,128)(2,1)} collective-permute-done((bf16[2,96,384]{2,1,0:T(8,128)(2,1)S(1)}, bf16[2,96,384]{2,1,0:T(8,128)(2,1)}, u32[]{:S(2)}, u32[]{:S(2)}) %collective-permute-start.8) | collective-permute-done | bytes 147488 | tf_op jit(solution)/shard_map/ppermute | solution.py:303
  27.6 11.9 %shard_map.55 = bf16[3,384,384]{2,1,0:T(8,128)(2,1)S(1)} custom-call(s32[26]{0:T(128)S(1)} %stack.56.place_ref, bf16[4,256,256]{2,1,0:T(8,128)(2,1)S(1)} %copy-done.1, f32[2,384,384]{2,1,0:T(8,128)S(1)} %bitcast.23, bf16[2,128,128]{2,1,0:T(8,128)(2,1)S(1)} %copy-done.2, bf16[9,128,128]{2,1,0:T(8,128)(2,1)S(1)} %pad_maximum_fusion.measured_own, ...), custom_call_target="tpu_custom_call" | custom-call | tf_op jit(solution)/shard_map/pallas_call | solution.py:309
  39.5 0.5 %collective-permute-start.13 = (bf16[3,384,384]{2,1,0:T(8,128)(2,1)S(1)}, bf16[3,384,384]{2,1,0:T(8,128)(2,1)S(1)}, u32[]{:S(2)}, u32[]{:S(2)}) collective-permute-start(bf16[3,384,384]{2,1,0:T(8,128)(2,1)S(1)} %shard_map.55), channel_id=1, source_target_pairs={{0,1},{1,0},{2,3},{3,2},{4,5},{5,4},{6,7},{7,6},{8,9},{9,8},{10,11... | collective-permute-start | bytes 2654216 | tf_op jit(solution)/shard_map/ppermute | solution.py:313
  40.0 2.1 %collective-permute-done.13 = bf16[3,384,384]{2,1,0:T(8,128)(2,1)S(1)} collective-permute-done((bf16[3,384,384]{2,1,0:T(8,128)(2,1)S(1)}, bf16[3,384,384]{2,1,0:T(8,128)(2,1)S(1)}, u32[]{:S(2)}, u32[]{:S(2)}) %collective-permute-start.13) | collective-permute-done | bytes 884768 | tf_op jit(solution)/shard_map/ppermute | solution.py:313
  42.0 0.2 convert_add_fusion
  42.2 0.1 fusion.3
  42.3 1.2 %fusion.1 = f32[2,1,384,384]{3,2,1,0:T(8,128)} fusion(f32[3,384,384]{2,1,0:T(8,128)S(1)} %convert_add_fusion, f32[384,384]{1,0:T(8,128)S(1)} %fusion.3, f32[2,1,384,384]{3,2,1,0:T(8,128)S(1)} %copy-done), kind=kLoop, calls=%fused_computation.3 | loop fusion | flops 589824 | bytes 4128768 | tf_op jit(solution)/shard_map/broadcast_in_dim | solution.py:316
  (13 shorter events, 0.1 us)
Async XLA Ops:
  0.0 5.1 %copy-start = (f32[2,1,384,384]{3,2,1,0:T(8,128)S(1)}, f32[2,1,384,384]{3,2,1,0:T(8,128)}, u32[]{:S(2)}) copy-start(f32[2,1,384,384]{3,2,1,0:T(8,128)} %param.5) | copy-start | bytes 3538948
  0.0 27.6 %copy-start.1 = (bf16[4,256,256]{2,1,0:T(8,128)(2,1)S(1)}, bf16[4,256,256]{2,1,0:T(8,128)(2,1)}, u32[]{:S(2)}) copy-start(bf16[4,256,256]{2,1,0:T(8,128)(2,1)} %constant.62.clone.tables_hbm) | copy-start | bytes 1572868
  0.0 27.6 %copy-start.2 = (bf16[2,128,128]{2,1,0:T(8,128)(2,1)S(1)}, bf16[2,128,128]{2,1,0:T(8,128)(2,1)}, u32[]{:S(2)}) copy-start(bf16[2,128,128]{2,1,0:T(8,128)(2,1)} %probe_hbm.1) | copy-start | bytes 196612
  2.0 13.7 %collective-permute-start.1 = (bf16[9,128,128]{2,1,0:T(8,128)(2,1)S(1)}, bf16[9,128,128]{2,1,0:T(8,128)(2,1)S(1)}, u32[]{:S(2)}, u32[]{:S(2)}) collective-permute-start(bf16[9,128,128]{2,1,0:T(8,128)(2,1)S(1)} %pad_maximum_fusion.measured_own), channel_id=1, source_target_pairs={{0,2},{1,3},{2,0},{3,1},{4,6},{5,7},{6,4},{7,5},{8,10},{9,11},{10,... | collective-permute-start | bytes 884744 | tf_op jit(solution)/shard_map/ppermute | solution.py:283
  5.1 9.5 %collective-permute-start.2 = (bf16[2,96,384]{2,1,0:T(8,128)(2,1)S(1)}, bf16[2,96,384]{2,1,0:T(8,128)(2,1)S(1)}, u32[]{:S(2)}, u32[]{:S(2)}) collective-permute-start(bf16[2,96,384]{2,1,0:T(8,128)(2,1)S(1)} %fusion.4), channel_id=1, source_target_pairs={{0,8},{4,12},{8,0},{12,4},{1,9},{5,13},{9,1},{13,5},{2,10},{6,14},... | collective-permute-start | bytes 442376 | tf_op jit(solution)/shard_map/ppermute | solution.py:291
  7.7 8.0 %collective-permute-start = (bf16[2,96,384]{2,1,0:T(8,128)(2,1)S(1)}, bf16[2,96,384]{2,1,0:T(8,128)(2,1)S(1)}, u32[]{:S(2)}, u32[]{:S(2)}) collective-permute-start(bf16[2,96,384]{2,1,0:T(8,128)(2,1)S(1)} %fusion.4), channel_id=1, source_target_pairs={{0,4},{4,0},{8,12},{12,8},{1,5},{5,1},{9,13},{13,9},{2,6},{6,2},{1... | collective-permute-start | bytes 442376 | tf_op jit(solution)/shard_map/ppermute | solution.py:291
  14.6 5.1 %collective-permute-start.3 = (bf16[2,96,384]{2,1,0:T(8,128)(2,1)S(1)}, bf16[2,96,384]{2,1,0:T(8,128)(2,1)S(1)}, u32[]{:S(2)}, u32[]{:S(2)}) collective-permute-start(bf16[2,96,384]{2,1,0:T(8,128)(2,1)S(1)} %collective-permute-done.2.rest_0_), channel_id=1, source_target_pairs={{0,2},{1,3},{2,0},{3,1},{4,6},{5,7},{6,4},{7,5},{8,10},{9,11},{10,... | collective-permute-start | bytes 442376 | tf_op jit(solution)/shard_map/ppermute | solution.py:292
  15.1 6.4 %collective-permute-start.9 = (bf16[2,96,384]{2,1,0:T(8,128)(2,1)S(1)}, bf16[2,96,384]{2,1,0:T(8,128)(2,1)S(1)}, u32[]{:S(2)}, u32[]{:S(2)}) collective-permute-start(bf16[2,96,384]{2,1,0:T(8,128)(2,1)S(1)} %collective-permute-done.2.rest_0_), channel_id=1, source_target_pairs={{0,4},{4,0},{8,12},{12,8},{1,5},{5,1},{9,13},{13,9},{2,6},{6,2},{1... | collective-permute-start | bytes 442376 | tf_op jit(solution)/shard_map/ppermute | solution.py:291
  15.7 6.3 %collective-permute-start.4 = (bf16[2,96,384]{2,1,0:T(8,128)(2,1)S(1)}, bf16[2,96,384]{2,1,0:T(8,128)(2,1)S(1)}, u32[]{:S(2)}, u32[]{:S(2)}) collective-permute-start(bf16[2,96,384]{2,1,0:T(8,128)(2,1)S(1)} %collective-permute-done.2.rest_0_), channel_id=1, source_target_pairs={{0,1},{1,0},{2,3},{3,2},{4,5},{5,4},{6,7},{7,6},{8,9},{9,8},{10,11... | collective-permute-start | bytes 442376 | tf_op jit(solution)/shard_map/ppermute | solution.py:302
  19.8 5.1 %collective-permute-start.10 = (bf16[2,96,384]{2,1,0:T(8,128)(2,1)S(1)}, bf16[2,96,384]{2,1,0:T(8,128)(2,1)S(1)}, u32[]{:S(2)}, u32[]{:S(2)}) collective-permute-start(bf16[2,96,384]{2,1,0:T(8,128)(2,1)S(1)} %collective-permute-done.3.rest_1_), channel_id=1, source_target_pairs={{0,4},{4,0},{8,12},{12,8},{1,5},{5,1},{9,13},{13,9},{2,6},{6,2},{1... | collective-permute-start | bytes 442376 | tf_op jit(solution)/shard_map/ppermute | solution.py:291
  21.0 5.1 %collective-permute-start.6 = (bf16[2,96,384]{2,1,0:T(8,128)(2,1)S(1)}, bf16[2,96,384]{2,1,0:T(8,128)(2,1)S(1)}, u32[]{:S(2)}, u32[]{:S(2)}) collective-permute-start(bf16[2,96,384]{2,1,0:T(8,128)(2,1)S(1)} %collective-permute-done.rest_4_), channel_id=1, source_target_pairs={{0,2},{1,3},{2,0},{3,1},{4,6},{5,7},{6,4},{7,5},{8,10},{9,11},{10,... | collective-permute-start | bytes 442376 | tf_op jit(solution)/shard_map/ppermute | solution.py:292
  21.5 4.7 %collective-permute-start.7 = (bf16[2,96,384]{2,1,0:T(8,128)(2,1)S(1)}, bf16[2,96,384]{2,1,0:T(8,128)(2,1)S(1)}, u32[]{:S(2)}, u32[]{:S(2)}) collective-permute-start(bf16[2,96,384]{2,1,0:T(8,128)(2,1)S(1)} %collective-permute-done.rest_4_), channel_id=1, source_target_pairs={{0,1},{1,0},{2,3},{3,2},{4,5},{5,4},{6,7},{7,6},{8,9},{9,8},{10,11... | collective-permute-start | bytes 442376 | tf_op jit(solution)/shard_map/ppermute | solution.py:302
  21.5 4.7 %collective-permute-start.5 = (bf16[2,96,384]{2,1,0:T(8,128)(2,1)S(1)}, bf16[2,96,384]{2,1,0:T(8,128)(2,1)}, u32[]{:S(2)}, u32[]{:S(2)}) collective-permute-start(bf16[2,96,384]{2,1,0:T(8,128)(2,1)S(1)} %collective-permute-done.3.rest_1_), channel_id=1, source_target_pairs={{0,1},{1,0},{2,3},{3,2},{4,5},{5,4},{6,7},{7,6},{8,9},{9,8},{10,11... | collective-permute-start | bytes 442376 | tf_op jit(solution)/shard_map/ppermute | solution.py:303
  22.0 4.2 %collective-permute-start.11 = (bf16[2,96,384]{2,1,0:T(8,128)(2,1)S(1)}, bf16[2,96,384]{2,1,0:T(8,128)(2,1)}, u32[]{:S(2)}, u32[]{:S(2)}) collective-permute-start(bf16[2,96,384]{2,1,0:T(8,128)(2,1)S(1)} %collective-permute-done.9.rest_8_), channel_id=1, source_target_pairs={{0,1},{1,0},{2,3},{3,2},{4,5},{5,4},{6,7},{7,6},{8,9},{9,8},{10,11... | collective-permute-start | bytes 442376 | tf_op jit(solution)/shard_map/ppermute | solution.py:302
  24.9 1.5 %collective-permute-start.12 = (bf16[2,96,384]{2,1,0:T(8,128)(2,1)S(1)}, bf16[2,96,384]{2,1,0:T(8,128)(2,1)}, u32[]{:S(2)}, u32[]{:S(2)}) collective-permute-start(bf16[2,96,384]{2,1,0:T(8,128)(2,1)S(1)} %collective-permute-done.10.rest_9_), channel_id=1, source_target_pairs={{0,1},{1,0},{2,3},{3,2},{4,5},{5,4},{6,7},{7,6},{8,9},{9,8},{10,11... | collective-permute-start | bytes 442376 | tf_op jit(solution)/shard_map/ppermute | solution.py:303
  26.1 1.5 %collective-permute-start.8 = (bf16[2,96,384]{2,1,0:T(8,128)(2,1)S(1)}, bf16[2,96,384]{2,1,0:T(8,128)(2,1)}, u32[]{:S(2)}, u32[]{:S(2)}) collective-permute-start(bf16[2,96,384]{2,1,0:T(8,128)(2,1)S(1)} %collective-permute-done.6.rest_5_), channel_id=1, source_target_pairs={{0,1},{1,0},{2,3},{3,2},{4,5},{5,4},{6,7},{7,6},{8,9},{9,8},{10,11... | collective-permute-start | bytes 442376 | tf_op jit(solution)/shard_map/ppermute | solution.py:303
  39.5 2.5 %collective-permute-start.13 = (bf16[3,384,384]{2,1,0:T(8,128)(2,1)S(1)}, bf16[3,384,384]{2,1,0:T(8,128)(2,1)S(1)}, u32[]{:S(2)}, u32[]{:S(2)}) collective-permute-start(bf16[3,384,384]{2,1,0:T(8,128)(2,1)S(1)} %shard_map.55), channel_id=1, source_target_pairs={{0,1},{1,0},{2,3},{3,2},{4,5},{5,4},{6,7},{7,6},{8,9},{9,8},{10,11... | collective-permute-start | bytes 2654216 | tf_op jit(solution)/shard_map/ppermute | solution.py:313

commit v4 on v3

--- a/solution.py
+++ b/solution.py
@@ -49,7 +49,17 @@
     rows = jnp.concatenate(
         [jnp.concatenate([re.astype(jnp.bfloat16), im.astype(jnp.bfloat16)], axis=1) for re, im in values], axis=0
     )
-    middle = jnp.dot(rows, right, preferred_element_type=jnp.float32).astype(jnp.bfloat16)
+    strips = math.gcd(len(values), 4)
+    height = rows.shape[0] // strips
+    middle = jnp.concatenate(
+        [
+            jnp.dot(rows[strip * height:(strip + 1) * height], right, preferred_element_type=jnp.float32).astype(
+                jnp.bfloat16
+            )
+            for strip in range(strips)
+        ],
+        axis=0,
+    )
     parts = [middle[index * extent:(index + 1) * extent] for index in range(len(values))]
     columns = jnp.concatenate(
         [
@@ -145,7 +155,7 @@
             waves[0, position, part] = pltpu.roll(probe_ref[part].astype(jnp.float32), shift, 1)
         return carry
 
-    lax.fori_loop(0, total, start_wave, 0, unroll=4)
+    lax.fori_loop(0, total, start_wave, 0, unroll=16)
     if resident:
         own_copy.wait()
         for part in range(2):
@@ -223,7 +233,7 @@
             sums[kind, second, pl.ds(row, extent), :] += jnp.where(mask, term, 0.0)
         return carry
 
-    lax.fori_loop(0, total, settle, 0)
+    lax.fori_loop(0, total, settle, 0, unroll=4)
     for kind in range(3):
         for block in range(blocks):
             out_ref[kind, :, block * lanes:(block + 1) * lanes] = sums[kind, block].astype(wire)

time: 43.7 us -> 42.7 us (0.977)
  Pallas kernels: 11.9 us -> 11 us
    pallas_call x1, Pallas kernels: 11.9 us -> 11 us  [on_device(): sums_call(sections, positions, extent, side, len(pieces), resident)]
where the time goes in v4:
time: 42.7 us; the launch traced here: 42.6 us
  waiting for transfers between devices  17.1 us (40%)
  Pallas kernels  11 us (26%)
  starting transfers between devices  10.7 us (25%)
  other arithmetic  3.38 us (8%)
    pallas_call x1, Pallas kernels, on_device(): sums_call(sections, positions, extent, side, len(pieces), resident)  11 us
    ppermute x4, waiting for transfers between devices, on_device(): go = lambda value, distance: lax.ppermute(value, 'cuts', swap(distance))  8.13 us
    ppermute x4, starting transfers between devices, on_device(): go = lambda value, distance: lax.ppermute(value, 'cuts', swap(distance))  6.04 us
    ppermute x2, waiting for transfers between devices, on_device(): over = lambda value: lax.ppermute(value, 'probe', across)  5.22 us
    ppermute x1, starting transfers between devices, on_device(): measured_other = lax.ppermute(measured, 'probe', across)  3.01 us
    ppermute x1, waiting for transfers between devices, on_device(): other_sums = lax.ppermute(own_sums, 'probe', beside)  2.41 us
    ppermute x3, waiting for transfers between devices, on_device(): lax.ppermute(opposite[distance], 'probe', beside)  1.37 us
    broadcast_in_dim x1, other arithmetic, on_device(): return updated[:, None]  1.2 us
  transfers between devices with their start and end apart: 14, of which 7 were waited for; matrix products, arithmetic and copies ran while one was open for 0% of the time, Pallas kernels for 0%

profile of v4, /device:TPU:0, one launch (start us, length us, event | category | flops | bytes accessed | tf_op | source)
XLA Modules:
  0.0 42.6 jit_solution(17654313598136425281)
XLA Ops:
  0.0 0.8 %convert_element_type.21 = bf16[8,2]{0,1:T(2,128)(2,1)S(1)} convert(s32[8,2]{0,1:T(2,128)} %param.8) | non-fusion elementwise | flops 16 | bytes 96 | tf_op jit(solution)/shard_map/convert_element_type | solution.py:291
  0.8 0.1 copy.9
  0.9 1.1 %convert_element_type.20 = bf16[8,128,128]{2,1,0:T(8,128)(2,1)S(1)} convert(f32[8,128,128]{2,1,0:T(8,128)} %param.7) | non-fusion elementwise | flops 131072 | bytes 786432 | tf_op jit(solution)/shard_map/convert_element_type | solution.py:292
  2.0 3.0 %collective-permute-start.1 = (bf16[9,128,128]{2,1,0:T(8,128)(2,1)S(1)}, bf16[9,128,128]{2,1,0:T(8,128)(2,1)S(1)}, u32[]{:S(2)}, u32[]{:S(2)}) collective-permute-start(bf16[9,128,128]{2,1,0:T(8,128)(2,1)S(1)} %pad_maximum_fusion.measured_own), channel_id=1, source_target_pairs={{0,2},{1,3},{2,0},{3,1},{4,6},{5,7},{6,4},{7,5},{8,10},{9,11},{10,... | collective-permute-start | bytes 884744 | tf_op jit(solution)/shard_map/ppermute | solution.py:293
  5.1 2.7 %collective-permute-start.2 = (bf16[2,96,384]{2,1,0:T(8,128)(2,1)S(1)}, bf16[2,96,384]{2,1,0:T(8,128)(2,1)S(1)}, u32[]{:S(2)}, u32[]{:S(2)}) collective-permute-start(bf16[2,96,384]{2,1,0:T(8,128)(2,1)S(1)} %fusion.4), channel_id=1, source_target_pairs={{0,8},{4,12},{8,0},{12,4},{1,9},{5,13},{9,1},{13,5},{2,10},{6,14},... | collective-permute-start | bytes 442376 | tf_op jit(solution)/shard_map/ppermute | solution.py:301
  7.7 1.6 %collective-permute-start = (bf16[2,96,384]{2,1,0:T(8,128)(2,1)S(1)}, bf16[2,96,384]{2,1,0:T(8,128)(2,1)S(1)}, u32[]{:S(2)}, u32[]{:S(2)}) collective-permute-start(bf16[2,96,384]{2,1,0:T(8,128)(2,1)S(1)} %fusion.4), channel_id=1, source_target_pairs={{0,4},{4,0},{8,12},{12,8},{1,5},{5,1},{9,13},{13,9},{2,6},{6,2},{1... | collective-permute-start | bytes 442376 | tf_op jit(solution)/shard_map/ppermute | solution.py:301
  9.3 5.3 %collective-permute-done.2.rest_0_ = bf16[2,96,384]{2,1,0:T(8,128)(2,1)S(1)} collective-permute-done((bf16[2,96,384]{2,1,0:T(8,128)(2,1)S(1)}, bf16[2,96,384]{2,1,0:T(8,128)(2,1)S(1)}, u32[]{:S(2)}, u32[]{:S(2)}) %collective-permute-start.2) | collective-permute-done | bytes 147488 | tf_op jit(solution)/shard_map/ppermute | solution.py:301
  14.6 0.5 %collective-permute-start.3 = (bf16[2,96,384]{2,1,0:T(8,128)(2,1)S(1)}, bf16[2,96,384]{2,1,0:T(8,128)(2,1)S(1)}, u32[]{:S(2)}, u32[]{:S(2)}) collective-permute-start(bf16[2,96,384]{2,1,0:T(8,128)(2,1)S(1)} %collective-permute-done.2.rest_0_), channel_id=1, source_target_pairs={{0,2},{1,3},{2,0},{3,1},{4,6},{5,7},{6,4},{7,5},{8,10},{9,11},{10,... | collective-permute-start | bytes 442376 | tf_op jit(solution)/shard_map/ppermute | solution.py:302
  15.1 0.6 %collective-permute-start.9 = (bf16[2,96,384]{2,1,0:T(8,128)(2,1)S(1)}, bf16[2,96,384]{2,1,0:T(8,128)(2,1)S(1)}, u32[]{:S(2)}, u32[]{:S(2)}) collective-permute-start(bf16[2,96,384]{2,1,0:T(8,128)(2,1)S(1)} %collective-permute-done.2.rest_0_), channel_id=1, source_target_pairs={{0,4},{4,0},{8,12},{12,8},{1,5},{5,1},{9,13},{13,9},{2,6},{6,2},{1... | collective-permute-start | bytes 442376 | tf_op jit(solution)/shard_map/ppermute | solution.py:301
  15.7 0.0 collective-permute-start.4
  15.7 0.0 collective-permute-done.rest_4_
  15.7 0.0 collective-permute-done.1.measured_other
  15.7 4.0 %collective-permute-done.3.rest_1_ = bf16[2,96,384]{2,1,0:T(8,128)(2,1)S(1)} collective-permute-done((bf16[2,96,384]{2,1,0:T(8,128)(2,1)S(1)}, bf16[2,96,384]{2,1,0:T(8,128)(2,1)S(1)}, u32[]{:S(2)}, u32[]{:S(2)}) %collective-permute-start.3) | collective-permute-done | bytes 147488 | tf_op jit(solution)/shard_map/ppermute | solution.py:302
  19.8 1.2 %collective-permute-start.10 = (bf16[2,96,384]{2,1,0:T(8,128)(2,1)S(1)}, bf16[2,96,384]{2,1,0:T(8,128)(2,1)S(1)}, u32[]{:S(2)}, u32[]{:S(2)}) collective-permute-start(bf16[2,96,384]{2,1,0:T(8,128)(2,1)S(1)} %collective-permute-done.3.rest_1_), channel_id=1, source_target_pairs={{0,4},{4,0},{8,12},{12,8},{1,5},{5,1},{9,13},{13,9},{2,6},{6,2},{1... | collective-permute-start | bytes 442376 | tf_op jit(solution)/shard_map/ppermute | solution.py:301
  21.0 0.5 %collective-permute-start.6 = (bf16[2,96,384]{2,1,0:T(8,128)(2,1)S(1)}, bf16[2,96,384]{2,1,0:T(8,128)(2,1)S(1)}, u32[]{:S(2)}, u32[]{:S(2)}) collective-permute-start(bf16[2,96,384]{2,1,0:T(8,128)(2,1)S(1)} %collective-permute-done.rest_4_), channel_id=1, source_target_pairs={{0,2},{1,3},{2,0},{3,1},{4,6},{5,7},{6,4},{7,5},{8,10},{9,11},{10,... | collective-permute-start | bytes 442376 | tf_op jit(solution)/shard_map/ppermute | solution.py:302
  21.5 0.0 collective-permute-start.7
  21.5 0.0 collective-permute-done.9.rest_8_
  21.5 0.5 %collective-permute-start.5 = (bf16[2,96,384]{2,1,0:T(8,128)(2,1)S(1)}, bf16[2,96,384]{2,1,0:T(8,128)(2,1)}, u32[]{:S(2)}, u32[]{:S(2)}) collective-permute-start(bf16[2,96,384]{2,1,0:T(8,128)(2,1)S(1)} %collective-permute-done.3.rest_1_), channel_id=1, source_target_pairs={{0,1},{1,0},{2,3},{3,2},{4,5},{5,4},{6,7},{7,6},{8,9},{9,8},{10,11... | collective-permute-start | bytes 442376 | tf_op jit(solution)/shard_map/ppermute | solution.py:313
  22.0 0.0 collective-permute-done.4.rest_2_
  22.0 0.1 collective-permute-start.11
  22.1 2.8 %collective-permute-done.10.rest_9_ = bf16[2,96,384]{2,1,0:T(8,128)(2,1)S(1)} collective-permute-done((bf16[2,96,384]{2,1,0:T(8,128)(2,1)S(1)}, bf16[2,96,384]{2,1,0:T(8,128)(2,1)S(1)}, u32[]{:S(2)}, u32[]{:S(2)}) %collective-permute-start.10) | collective-permute-done | bytes 147488 | tf_op jit(solution)/shard_map/ppermute | solution.py:301
  24.9 1.2 %collective-permute-done.6.rest_5_ = bf16[2,96,384]{2,1,0:T(8,128)(2,1)S(1)} collective-permute-done((bf16[2,96,384]{2,1,0:T(8,128)(2,1)S(1)}, bf16[2,96,384]{2,1,0:T(8,128)(2,1)S(1)}, u32[]{:S(2)}, u32[]{:S(2)}) %collective-permute-start.6) | collective-permute-done | bytes 147488 | tf_op jit(solution)/shard_map/ppermute | solution.py:302
  26.1 0.0 collective-permute-start.8
  26.1 0.1 stack.56.place_ref
  26.2 0.2 collective-permute-done.12.rest_11_
  26.4 1.2 %collective-permute-done.8.rest_7_ = bf16[2,96,384]{2,1,0:T(8,128)(2,1)} collective-permute-done((bf16[2,96,384]{2,1,0:T(8,128)(2,1)S(1)}, bf16[2,96,384]{2,1,0:T(8,128)(2,1)}, u32[]{:S(2)}, u32[]{:S(2)}) %collective-permute-start.8) | collective-permute-done | bytes 147488 | tf_op jit(solution)/shard_map/ppermute | solution.py:313
  27.6 11.0 %shard_map.55 = bf16[3,384,384]{2,1,0:T(8,128)(2,1)S(1)} custom-call(s32[26]{0:T(128)S(1)} %stack.56.place_ref, bf16[4,256,256]{2,1,0:T(8,128)(2,1)S(1)} %copy-done.1, f32[2,384,384]{2,1,0:T(8,128)S(1)} %bitcast.23, bf16[2,128,128]{2,1,0:T(8,128)(2,1)S(1)} %copy-done.2, bf16[9,128,128]{2,1,0:T(8,128)(2,1)S(1)} %pad_maximum_fusion.measured_own, ...), custom_call_target="tpu_custom_call" | custom-call | tf_op jit(solution)/shard_map/pallas_call | solution.py:319
  38.6 0.1 collective-permute-start.13
  38.7 2.4 %collective-permute-done.13 = bf16[3,384,384]{2,1,0:T(8,128)(2,1)S(1)} collective-permute-done((bf16[3,384,384]{2,1,0:T(8,128)(2,1)S(1)}, bf16[3,384,384]{2,1,0:T(8,128)(2,1)S(1)}, u32[]{:S(2)}, u32[]{:S(2)}) %collective-permute-start.13) | collective-permute-done | bytes 884768 | tf_op jit(solution)/shard_map/ppermute | solution.py:323
  41.1 0.2 convert_add_fusion
  41.3 0.1 fusion.3
  41.4 1.2 %fusion.1 = f32[2,1,384,384]{3,2,1,0:T(8,128)} fusion(f32[3,384,384]{2,1,0:T(8,128)S(1)} %convert_add_fusion, f32[384,384]{1,0:T(8,128)S(1)} %fusion.3, f32[2,1,384,384]{3,2,1,0:T(8,128)S(1)} %copy-done), kind=kLoop, calls=%fused_computation.3 | loop fusion | flops 589824 | bytes 4128768 | tf_op jit(solution)/shard_map/broadcast_in_dim | solution.py:326
  (13 shorter events, 0.1 us)
Async XLA Ops:
  0.0 5.1 %copy-start = (f32[2,1,384,384]{3,2,1,0:T(8,128)S(1)}, f32[2,1,384,384]{3,2,1,0:T(8,128)}, u32[]{:S(2)}) copy-start(f32[2,1,384,384]{3,2,1,0:T(8,128)} %param.5) | copy-start | bytes 3538948
  0.0 27.6 %copy-start.1 = (bf16[4,256,256]{2,1,0:T(8,128)(2,1)S(1)}, bf16[4,256,256]{2,1,0:T(8,128)(2,1)}, u32[]{:S(2)}) copy-start(bf16[4,256,256]{2,1,0:T(8,128)(2,1)} %constant.62.clone.tables_hbm) | copy-start | bytes 1572868
  0.0 27.6 %copy-start.2 = (bf16[2,128,128]{2,1,0:T(8,128)(2,1)S(1)}, bf16[2,128,128]{2,1,0:T(8,128)(2,1)}, u32[]{:S(2)}) copy-start(bf16[2,128,128]{2,1,0:T(8,128)(2,1)} %probe_hbm.1) | copy-start | bytes 196612
  2.0 13.7 %collective-permute-start.1 = (bf16[9,128,128]{2,1,0:T(8,128)(2,1)S(1)}, bf16[9,128,128]{2,1,0:T(8,128)(2,1)S(1)}, u32[]{:S(2)}, u32[]{:S(2)}) collective-permute-start(bf16[9,128,128]{2,1,0:T(8,128)(2,1)S(1)} %pad_maximum_fusion.measured_own), channel_id=1, source_target_pairs={{0,2},{1,3},{2,0},{3,1},{4,6},{5,7},{6,4},{7,5},{8,10},{9,11},{10,... | collective-permute-start | bytes 884744 | tf_op jit(solution)/shard_map/ppermute | solution.py:293
  5.1 9.5 %collective-permute-start.2 = (bf16[2,96,384]{2,1,0:T(8,128)(2,1)S(1)}, bf16[2,96,384]{2,1,0:T(8,128)(2,1)S(1)}, u32[]{:S(2)}, u32[]{:S(2)}) collective-permute-start(bf16[2,96,384]{2,1,0:T(8,128)(2,1)S(1)} %fusion.4), channel_id=1, source_target_pairs={{0,8},{4,12},{8,0},{12,4},{1,9},{5,13},{9,1},{13,5},{2,10},{6,14},... | collective-permute-start | bytes 442376 | tf_op jit(solution)/shard_map/ppermute | solution.py:301
  7.7 8.0 %collective-permute-start = (bf16[2,96,384]{2,1,0:T(8,128)(2,1)S(1)}, bf16[2,96,384]{2,1,0:T(8,128)(2,1)S(1)}, u32[]{:S(2)}, u32[]{:S(2)}) collective-permute-start(bf16[2,96,384]{2,1,0:T(8,128)(2,1)S(1)} %fusion.4), channel_id=1, source_target_pairs={{0,4},{4,0},{8,12},{12,8},{1,5},{5,1},{9,13},{13,9},{2,6},{6,2},{1... | collective-permute-start | bytes 442376 | tf_op jit(solution)/shard_map/ppermute | solution.py:301
  14.6 5.1 %collective-permute-start.3 = (bf16[2,96,384]{2,1,0:T(8,128)(2,1)S(1)}, bf16[2,96,384]{2,1,0:T(8,128)(2,1)S(1)}, u32[]{:S(2)}, u32[]{:S(2)}) collective-permute-start(bf16[2,96,384]{2,1,0:T(8,128)(2,1)S(1)} %collective-permute-done.2.rest_0_), channel_id=1, source_target_pairs={{0,2},{1,3},{2,0},{3,1},{4,6},{5,7},{6,4},{7,5},{8,10},{9,11},{10,... | collective-permute-start | bytes 442376 | tf_op jit(solution)/shard_map/ppermute | solution.py:302
  15.1 6.4 %collective-permute-start.9 = (bf16[2,96,384]{2,1,0:T(8,128)(2,1)S(1)}, bf16[2,96,384]{2,1,0:T(8,128)(2,1)S(1)}, u32[]{:S(2)}, u32[]{:S(2)}) collective-permute-start(bf16[2,96,384]{2,1,0:T(8,128)(2,1)S(1)} %collective-permute-done.2.rest_0_), channel_id=1, source_target_pairs={{0,4},{4,0},{8,12},{12,8},{1,5},{5,1},{9,13},{13,9},{2,6},{6,2},{1... | collective-permute-start | bytes 442376 | tf_op jit(solution)/shard_map/ppermute | solution.py:301
  15.7 6.3 %collective-permute-start.4 = (bf16[2,96,384]{2,1,0:T(8,128)(2,1)S(1)}, bf16[2,96,384]{2,1,0:T(8,128)(2,1)S(1)}, u32[]{:S(2)}, u32[]{:S(2)}) collective-permute-start(bf16[2,96,384]{2,1,0:T(8,128)(2,1)S(1)} %collective-permute-done.2.rest_0_), channel_id=1, source_target_pairs={{0,1},{1,0},{2,3},{3,2},{4,5},{5,4},{6,7},{7,6},{8,9},{9,8},{10,11... | collective-permute-start | bytes 442376 | tf_op jit(solution)/shard_map/ppermute | solution.py:312
  19.8 5.1 %collective-permute-start.10 = (bf16[2,96,384]{2,1,0:T(8,128)(2,1)S(1)}, bf16[2,96,384]{2,1,0:T(8,128)(2,1)S(1)}, u32[]{:S(2)}, u32[]{:S(2)}) collective-permute-start(bf16[2,96,384]{2,1,0:T(8,128)(2,1)S(1)} %collective-permute-done.3.rest_1_), channel_id=1, source_target_pairs={{0,4},{4,0},{8,12},{12,8},{1,5},{5,1},{9,13},{13,9},{2,6},{6,2},{1... | collective-permute-start | bytes 442376 | tf_op jit(solution)/shard_map/ppermute | solution.py:301
  21.0 5.1 %collective-permute-start.6 = (bf16[2,96,384]{2,1,0:T(8,128)(2,1)S(1)}, bf16[2,96,384]{2,1,0:T(8,128)(2,1)S(1)}, u32[]{:S(2)}, u32[]{:S(2)}) collective-permute-start(bf16[2,96,384]{2,1,0:T(8,128)(2,1)S(1)} %collective-permute-done.rest_4_), channel_id=1, source_target_pairs={{0,2},{1,3},{2,0},{3,1},{4,6},{5,7},{6,4},{7,5},{8,10},{9,11},{10,... | collective-permute-start | bytes 442376 | tf_op jit(solution)/shard_map/ppermute | solution.py:302
  21.5 4.7 %collective-permute-start.7 = (bf16[2,96,384]{2,1,0:T(8,128)(2,1)S(1)}, bf16[2,96,384]{2,1,0:T(8,128)(2,1)S(1)}, u32[]{:S(2)}, u32[]{:S(2)}) collective-permute-start(bf16[2,96,384]{2,1,0:T(8,128)(2,1)S(1)} %collective-permute-done.rest_4_), channel_id=1, source_target_pairs={{0,1},{1,0},{2,3},{3,2},{4,5},{5,4},{6,7},{7,6},{8,9},{9,8},{10,11... | collective-permute-start | bytes 442376 | tf_op jit(solution)/shard_map/ppermute | solution.py:312
  21.5 4.7 %collective-permute-start.5 = (bf16[2,96,384]{2,1,0:T(8,128)(2,1)S(1)}, bf16[2,96,384]{2,1,0:T(8,128)(2,1)}, u32[]{:S(2)}, u32[]{:S(2)}) collective-permute-start(bf16[2,96,384]{2,1,0:T(8,128)(2,1)S(1)} %collective-permute-done.3.rest_1_), channel_id=1, source_target_pairs={{0,1},{1,0},{2,3},{3,2},{4,5},{5,4},{6,7},{7,6},{8,9},{9,8},{10,11... | collective-permute-start | bytes 442376 | tf_op jit(solution)/shard_map/ppermute | solution.py:313
  22.0 4.2 %collective-permute-start.11 = (bf16[2,96,384]{2,1,0:T(8,128)(2,1)S(1)}, bf16[2,96,384]{2,1,0:T(8,128)(2,1)}, u32[]{:S(2)}, u32[]{:S(2)}) collective-permute-start(bf16[2,96,384]{2,1,0:T(8,128)(2,1)S(1)} %collective-permute-done.9.rest_8_), channel_id=1, source_target_pairs={{0,1},{1,0},{2,3},{3,2},{4,5},{5,4},{6,7},{7,6},{8,9},{9,8},{10,11... | collective-permute-start | bytes 442376 | tf_op jit(solution)/shard_map/ppermute | solution.py:312
  24.9 1.5 %collective-permute-start.12 = (bf16[2,96,384]{2,1,0:T(8,128)(2,1)S(1)}, bf16[2,96,384]{2,1,0:T(8,128)(2,1)}, u32[]{:S(2)}, u32[]{:S(2)}) collective-permute-start(bf16[2,96,384]{2,1,0:T(8,128)(2,1)S(1)} %collective-permute-done.10.rest_9_), channel_id=1, source_target_pairs={{0,1},{1,0},{2,3},{3,2},{4,5},{5,4},{6,7},{7,6},{8,9},{9,8},{10,11... | collective-permute-start | bytes 442376 | tf_op jit(solution)/shard_map/ppermute | solution.py:313
  26.1 1.5 %collective-permute-start.8 = (bf16[2,96,384]{2,1,0:T(8,128)(2,1)S(1)}, bf16[2,96,384]{2,1,0:T(8,128)(2,1)}, u32[]{:S(2)}, u32[]{:S(2)}) collective-permute-start(bf16[2,96,384]{2,1,0:T(8,128)(2,1)S(1)} %collective-permute-done.6.rest_5_), channel_id=1, source_target_pairs={{0,1},{1,0},{2,3},{3,2},{4,5},{5,4},{6,7},{7,6},{8,9},{9,8},{10,11... | collective-permute-start | bytes 442376 | tf_op jit(solution)/shard_map/ppermute | solution.py:313
  38.6 2.5 %collective-permute-start.13 = (bf16[3,384,384]{2,1,0:T(8,128)(2,1)S(1)}, bf16[3,384,384]{2,1,0:T(8,128)(2,1)S(1)}, u32[]{:S(2)}, u32[]{:S(2)}) collective-permute-start(bf16[3,384,384]{2,1,0:T(8,128)(2,1)S(1)} %shard_map.55), channel_id=1, source_target_pairs={{0,1},{1,0},{2,3},{3,2},{4,5},{5,4},{6,7},{7,6},{8,9},{9,8},{10,11... | collective-permute-start | bytes 2654216 | tf_op jit(solution)/shard_map/ppermute | solution.py:323
